TPU v7x, 256 devices: a whole 4x4x8 slice. The times are simulated.
256 devices in a mesh: row: 64 (over y, z_lo, x, core), col: 4 (over z_hi).
Axes of the slice: x: 4, y: 4, z: 8 (z_hi: 4, z_lo: 2; z = z_hi * 2 + z_lo), core: 2. Of those that a mesh axis runs over, the one named last changes fastest.
Arguments:
- tokens: bfloat16 [1536, 128, 128], P('row', 'col'), may hold values from -6 to 6
- attn_gain: float32 [2, 128], replicated, may hold values from 0.1 to 1.9
- w_qkv: bfloat16 [2, 128, 384], replicated, may hold values from -0.5 to 0.5
- score_scale: float32 [2, 2], replicated, may hold values from 2 to 10
- w_out: bfloat16 [2, 128, 128], replicated, may hold values from -0.5 to 0.5
- mlp_gain: float32 [2, 128], replicated, may hold values from 0.1 to 1.9
- w_in: bfloat16 [2, 128, 768], replicated, may hold values from -0.5 to 0.5
- down_weight: bfloat16 [2, 384, 128], replicated, may hold values from -0.3125 to 0.3125
Outputs:
- result: bfloat16 [1536, 128, 128], P('row', 'col')
All inputs are finite; a program needn't handle non-finite values.
Results may differ from a plain program's by a relative error of at most 0.025.
Values may be sent and summed in bfloat16 or wider, within the bound.
A program may use at most 128 MiB of HBM per device.

v0:
```python
import jax
import jax.numpy as jnp
from jax import lax
from jax.sharding import PartitionSpec as P

WIN = 7
SECOND_DILATION = 8
LAYERS = 2


def with_halo(value, sides, width):
    for axis, dim in sides:
        count, length = (lax.axis_size(axis), value.shape[dim])
        up = [(i, (i + 1) % count) for i in range(count - 1)]
        down = [(j, i) for i, j in up]
        last = lax.slice_in_dim(value, length - width, length, axis=dim)
        leading = lax.slice_in_dim(value, 0, width, axis=dim)
        before = lax.ppermute(last, axis, up)
        after = lax.ppermute(leading, axis, down)
        value = jnp.concatenate([before, value, after], axis=dim)
    return value


def norm_rows(values, gain):
    floats = values.astype(jnp.float32)
    scale = lax.rsqrt(jnp.mean(floats * floats, axis=-1, keepdims=True) + 1e-06)
    return (floats * scale * gain).astype(jnp.bfloat16)


def project_rows(normed, weight):
    rows, cols, width = normed.shape
    product = jnp.dot(
        normed.reshape(rows * cols, width), weight, preferred_element_type=jnp.float32
    )
    return product.astype(jnp.bfloat16).reshape(rows, cols, weight.shape[1])


def local_window_attend(query, keyval, valid, scale, dilation_step, window, heads):
    rows, cols, width = query.shape
    size = width // heads
    query_f = query.astype(jnp.float32).reshape(rows, cols, heads, size)
    query_unit = (
        query_f
        * lax.rsqrt(jnp.sum(query_f * query_f, axis=-1, keepdims=True) + 1e-06)
        * scale[:, None]
    )
    big_rows, big_cols = (keyval.shape[0], keyval.shape[1])
    keys = keyval[:, :, :width].reshape(big_rows, big_cols, heads, size)
    vals = keyval[:, :, width:].reshape(big_rows, big_cols, heads, size)
    keys_f = keys.astype(jnp.float32)
    key_inv = lax.rsqrt(jnp.sum(keys_f * keys_f, axis=-1) + 1e-06)
    numer = jnp.zeros((rows, cols, heads, size), jnp.float32)
    denom = jnp.zeros((rows, cols, heads), jnp.float32)
    for step_a in range(window):
        for step_b in range(window):
            top = step_a * dilation_step
            left = step_b * dilation_step
            key_part = keys[top : top + rows, left : left + cols].astype(jnp.float32)
            score = (
                jnp.sum(query_unit * key_part, axis=-1)
                * key_inv[top : top + rows, left : left + cols]
            )
            weight = jnp.exp(score) * valid[top : top + rows, left : left + cols, None]
            denom = denom + weight
            numer = numer + weight[..., None] * vals[top : top + rows, left : left + cols].astype(
                jnp.float32
            )
    attended = numer / denom[..., None]
    return attended.reshape(rows, cols, width).astype(jnp.bfloat16)


def finish_layer(values, attended, w_out, mlp_gain, w_in, down_weight):
    rows, cols, width = values.shape
    hidden_ff = down_weight.shape[0]
    proj = jnp.dot(attended.reshape(rows * cols, width), w_out, preferred_element_type=jnp.float32)
    first = (values.astype(jnp.float32) + proj.reshape(rows, cols, width)).astype(jnp.bfloat16)
    normed = norm_rows(first, mlp_gain)
    inner = jnp.dot(normed.reshape(rows * cols, width), w_in, preferred_element_type=jnp.float32)
    hidden = (inner[:, :hidden_ff] * jax.nn.gelu(inner[:, hidden_ff:], approximate=True)).astype(
        jnp.bfloat16
    )
    down = jnp.dot(hidden, down_weight, preferred_element_type=jnp.float32).reshape(
        rows, cols, width
    )
    return (first.astype(jnp.float32) + down).astype(jnp.bfloat16)


def shards(tokens, attn_gain, w_qkv, score_scale, w_out, mlp_gain, w_in, down_weight):
    rows, cols, width = tokens.shape
    heads = score_scale.shape[1]
    window = WIN
    total_rows = rows * lax.axis_size("row")
    total_cols = cols * lax.axis_size("col")
    first_row = lax.axis_index("row") * rows
    col_start = lax.axis_index("col") * cols
    values = tokens
    for layer_index in range(LAYERS):
        dilation_step = 1 if layer_index == 0 else SECOND_DILATION
        reach = window // 2 * dilation_step
        normed = norm_rows(values, attn_gain[layer_index])
        if layer_index == 0:
            stacked = project_rows(normed, w_qkv[layer_index])
            query = stacked[:, :, :width]
            keyval = with_halo(stacked[:, :, width:], (("row", 0), ("col", 1)), reach)
        else:
            stacked = project_rows(normed, w_qkv[layer_index])
            query = stacked[:, :, :width]
            keyval = with_halo(stacked[:, :, width:], (("row", 0), ("col", 1)), reach)
        row_ids = first_row - reach + jnp.arange(rows + 2 * reach, dtype=jnp.int32)
        col_ids = col_start - reach + jnp.arange(cols + 2 * reach, dtype=jnp.int32)
        row_inside = (row_ids >= 0) & (row_ids < total_rows)
        col_ok = (col_ids >= 0) & (col_ids < total_cols)
        valid = (row_inside[:, None] & col_ok[None, :]).astype(jnp.float32)
        attended = local_window_attend(
            query, keyval, valid, score_scale[layer_index], dilation_step, window, heads
        )
        values = finish_layer(
            values,
            attended,
            w_out[layer_index],
            mlp_gain[layer_index],
            w_in[layer_index],
            down_weight[layer_index],
        )
    return values


def solution(mesh):
    return jax.shard_map(
        shards,
        mesh=mesh,
        in_specs=(P("row", "col", None), P(), P(), P(), P(), P(), P(), P()),
        out_specs=P("row", "col", None),
        check_vma=False,
    )
```

profile of v0, /device:TPU:24, one launch (start us, length us, event | category | flops | bytes accessed | tf_op | source)
XLA Modules:
  0.0 302.3 jit_solution(11426706126244631133)
XLA Ops:
  0.0 1.3 slice_bitcast_fusion.2
  1.3 1.1 fusion.26
  2.5 1.1 fusion.28
  3.6 1.2 convolution_convert_fusion.1
  4.8 1.9 collective-permute-start
  6.7 6.7 %collective-permute-start.1 = (bf16[3,32,256]{2,1,0:T(8,128)(2,1)S(1)}, bf16[3,32,256]{2,1,0:T(8,128)(2,1)S(1)}, u32[]{:S(2)}, u32[]{:S(2)}) collective-permute-start(bf16[3,32,256]{2,1,0:T(8,128)(2,1)S(1)} %get-tuple-element.210), channel_id=1, source_target_pairs={{4,0},{8,4},{12,8},{16,12},{20,16},{24,20},{28,24},{32,28},{36,32}... | collective-permute-start | bytes 147464 | tf_op jit(solution)/shard_map/ppermute | solution.py:19
  13.7 0.8 fusion.350
  15.0 0.9 multiply_reduce_fusion.101
  16.2 0.6 slice_bitcast_fusion
  16.7 0.6 compare_and_fusion.1
  17.4 5.2 %collective-permute-start.2 = (bf16[30,3,256]{2,1,0:T(4,128)(2,1)S(1)}, bf16[30,3,256]{2,1,0:T(4,128)(2,1)S(1)}, u32[]{:S(2)}, u32[]{:S(2)}) collective-permute-start(bf16[30,3,256]{2,1,0:T(4,128)(2,1)S(1)} %get-tuple-element.211), channel_id=1, source_target_pairs={{0,1},{1,2},{2,3},{4,5},{5,6},{6,7},{8,9},{9,10},{10,11},{12,13},{... | collective-permute-start | bytes 138248 | tf_op jit(solution)/shard_map/ppermute | solution.py:18
  22.6 1.7 collective-permute-start.3
  24.3 0.5 compare_and_fusion
  25.0 6.5 %collective-permute-done.3 = bf16[30,3,256]{2,1,0:T(4,128)(2,1)S(1)} collective-permute-done((bf16[30,3,256]{2,1,0:T(4,128)(2,1)S(1)}, bf16[30,3,256]{2,1,0:T(4,128)(2,1)S(1)}, u32[]{:S(2)}, u32[]{:S(2)}) %collective-permute-start.3) | collective-permute-done | bytes 46112 | tf_op jit(solution)/shard_map/ppermute | solution.py:19
  32.4 14.9 %multiply_reduce_fusion.98 = (f32[24,32,2]{2,1,0:T(8,128)}, f32[24,32,2]{2,1,0:T(8,128)}, f32[24,32,2]{2,1,0:T(8,128)}, f32[24,32,2]{2,1,0:T(8,128)}, f32[24,32,...) fusion(bf16[30,38,2,64]{3,2,1,0:T(2,128)(2,1)S(1)} %reshape.340, ...), kind=kLoop, calls=%fused_computation.136 | loop fusion | flops 4010496 | bytes 3428360 | tf_op jit(solution)/shard_map/reduce_sum | solution.py:60
  47.3 18.6 %multiply_reduce_fusion.100 = (f32[24,32,2]{2,1,0:T(8,128)}, f32[24,32,2]{2,1,0:T(8,128)}, f32[24,32,2]{2,1,0:T(8,128)}, f32[24,32,2]{2,1,0:T(8,128)}, f32[24,32...) fusion(f32[24,32,2,64]{3,2,1,0:T(2,128)S(1)} %get-tuple-element, ...), kind=kLoop, calls=%fused_computation.138 | loop fusion | flops 5280768 | bytes 4042752 | tf_op jit(solution)/shard_map/reduce_sum | solution.py:60
  65.9 18.7 %multiply_reduce_fusion.99 = (f32[24,32,2]{2,1,0:T(8,128)}, f32[24,32,2]{2,1,0:T(8,128)}, f32[24,32,2]{2,1,0:T(8,128)}, f32[24,32,2]{2,1,0:T(8,128)}, f32[24,32,...) fusion(f32[24,32,2,64]{3,2,1,0:T(2,128)S(1)} %get-tuple-element, ...), kind=kLoop, calls=%fused_computation.137 | loop fusion | flops 5280768 | bytes 4042752 | tf_op jit(solution)/shard_map/reduce_sum | solution.py:60
  84.6 1.3 multiply_reduce_fusion.51
  86.2 13.4 %add_add_fusion = (f32[24,32,2]{2,1,0:T(8,128)S(1)}, f32[24,32,2]{2,1,0:T(8,128)S(1)}, f32[24,32,2]{2,1,0:T(8,128)S(1)}, f32[24,32,2]{2,1,0:T(8,128)S(1)}, f32[2...) fusion(f32[24,32]{1,0:T(8,128)S(1)} %get-tuple-element.309, ...), kind=kLoop, calls=%fused_computation.302 | loop fusion | flops 224256 | bytes 1059840 | tf_op jit(solution)/shard_map/add | solution.py:64
  99.7 83.0 %fusion.25 = bf16[24,32,2,64]{3,2,1,0:T(2,128)(2,1)S(1)} fusion(bf16[30,38,2,64]{3,2,1,0:T(2,128)(2,1)S(1)} %reshape.341, f32[24,32,2]{2,1,0:T(8,128)S(1)} %get-tuple-element.152, f32[24,32,2]{2,1,0:T(8,128)} %get-tuple-element.201, f32[24,32,2]{2,1,0:T(8,128)} %get-tuple-element.200, f32[24,32,2]{2,1,0:T(8,128)} %get-tuple-element.199, ...), kind=kLoop, calls=%fused_computation.141 | loop fusion | flops 14548992 | bytes 10137600 | tf_op jit(solution)/shard_map/convert_element_type | solution.py:69
  186.1 1.9 collective-permute-start.4
  188.0 6.7 %collective-permute-start.5 = (bf16[24,32,256]{2,1,0:T(8,128)(2,1)S(1)}, bf16[24,32,256]{2,1,0:T(8,128)(2,1)S(1)}, u32[]{:S(2)}, u32[]{:S(2)}) collective-permute-start(bf16[24,32,256]{2,1,0:T(8,128)(2,1)S(1)} %slice.1903), channel_id=1, source_target_pairs={{4,0},{8,4},{12,8},{16,12},{20,16},{24,20},{28,24},{32,28},{36,32}... | collective-permute-start | bytes 1179656 | tf_op jit(solution)/shard_map/ppermute | solution.py:19
  194.7 0.8 fusion.346
  195.6 2.6 collective-permute-done.4
  198.2 1.8 collective-permute-done.5
  200.1 1.3 fusion.343
  201.4 6.8 %collective-permute-start.6 = (bf16[72,24,256]{2,1,0:T(8,128)(2,1)}, bf16[72,24,256]{2,1,0:T(8,128)(2,1)}, u32[]{:S(2)}, u32[]{:S(2)}) collective-permute-start(bf16[72,24,256]{2,1,0:T(8,128)(2,1)} %get-tuple-element.205), channel_id=1, source_target_pairs={{0,1},{1,2},{2,3},{4,5},{5,6},{6,7},{8,9},{9,10},{10,11},{12,13},{... | collective-permute-start | bytes 2654216 | tf_op jit(solution)/shard_map/ppermute | solution.py:18
  208.2 1.3 collective-permute-start.7
  209.4 0.7 fusion.348
  210.2 0.8 fusion.347
  211.0 0.5 copy.28
  211.8 3.3 %copy.32 = bf16[72,32,256]{1,2,0:T(8,128)(2,1)} copy(bf16[72,32,256]{2,1,0:T(8,128)(2,1)S(1)} %pad_maximum_fusion.1) | data formatting | bytes 2359296 | tf_op jit(solution)/shard_map/concatenate | solution.py:20
  215.1 8.1 %collective-permute-done.6 = bf16[72,24,256]{2,1,0:T(8,128)(2,1)} collective-permute-done((bf16[72,24,256]{2,1,0:T(8,128)(2,1)}, bf16[72,24,256]{2,1,0:T(8,128)(2,1)}, u32[]{:S(2)}, u32[]{:S(2)}) %collective-permute-start.6) | collective-permute-done | bytes 884768 | tf_op jit(solution)/shard_map/ppermute | solution.py:18
  223.2 4.8 %copy.31 = bf16[72,24,256]{1,2,0:T(8,128)(2,1)} copy(bf16[72,24,256]{2,1,0:T(8,128)(2,1)} %collective-permute-done.6) | data formatting | bytes 1769472 | tf_op jit(solution)/shard_map/ppermute | solution.py:18
  228.0 18.6 %collective-permute-done.7 = bf16[72,24,256]{2,1,0:T(8,128)(2,1)} collective-permute-done((bf16[72,24,256]{2,1,0:T(8,128)(2,1)}, bf16[72,24,256]{2,1,0:T(8,128)(2,1)}, u32[]{:S(2)}, u32[]{:S(2)}) %collective-permute-start.7) | collective-permute-done | bytes 884768 | tf_op jit(solution)/shard_map/ppermute | solution.py:19
  246.6 4.7 %copy.33 = bf16[72,24,256]{1,2,0:T(8,128)(2,1)} copy(bf16[72,24,256]{2,1,0:T(8,128)(2,1)} %collective-permute-done.7) | data formatting | bytes 1769472 | tf_op jit(solution)/shard_map/ppermute | solution.py:19
  251.3 7.4 %pad_maximum_fusion = bf16[72,80,256]{1,2,0:T(8,128)(2,1)S(1)} fusion(bf16[72,24,256]{1,2,0:T(8,128)(2,1)} %copy.33, bf16[72,32,256]{1,2,0:T(8,128)(2,1)} %copy.32, bf16[72,24,256]{1,2,0:T(8,128)(2,1)} %copy.31), kind=kLoop, calls=%fused_computation | loop fusion | flops 8847360 | bytes 5898240 | tf_op jit(solution)/shard_map/concatenate | solution.py:20
  258.8 1.4 fusion.342
  260.1 0.6 multiply_reduce_fusion.1
  260.7 6.5 %multiply_reduce_fusion.47 = (f32[24,32,2]{1,2,0:T(2,128)S(1)}, f32[24,32,2]{1,2,0:T(2,128)S(1)}, f32[24,32,2]{1,2,0:T(2,128)S(1)}, f32[24,32,2]{1,2,0:T(2,128)S...) fusion(bf16[72,80,2,64]{1,3,2,0:T(8,128)(2,1)S(1)} %bitcast.168, ...), kind=kLoop, calls=%fused_computation.51 | loop fusion | flops 4890624 | bytes 3643400 | tf_op jit(solution)/shard_map/reduce_sum | solution.py:60
  267.2 6.4 %multiply_reduce_fusion.49 = (f32[24,32,2]{1,2,0:T(2,128)S(1)}, f32[24,32,2]{1,2,0:T(2,128)S(1)}, f32[24,32,2]{1,2,0:T(2,128)S(1)}, f32[24,32,2]{1,2,0:T(2,128)S...) fusion(bf16[72,80,2,64]{1,3,2,0:T(8,128)(2,1)S(1)} %bitcast.169, ...), kind=kLoop, calls=%fused_computation.53 | loop fusion | flops 4890624 | bytes 3643400 | tf_op jit(solution)/shard_map/reduce_sum | solution.py:60
  273.6 6.9 %multiply_reduce_fusion.48 = (f32[24,32,2]{1,2,0:T(2,128)S(1)}, f32[24,32,2]{1,2,0:T(2,128)S(1)}, f32[24,32,2]{1,2,0:T(2,128)S(1)}, f32[24,32,2]{1,2,0:T(2,128)S...) fusion(bf16[72,80,2,64]{1,3,2,0:T(8,128)(2,1)S(1)} %bitcast.170, ...), kind=kLoop, calls=%fused_computation.52 | loop fusion | flops 4890624 | bytes 3643400 | tf_op jit(solution)/shard_map/reduce_sum | solution.py:60
  280.9 1.0 multiply_reduce_fusion
  282.4 3.2 %add_add_fusion.1 = (f32[24,32,2]{1,2,0:T(2,128)S(1)}, f32[24,32,2]{1,2,0:T(2,128)S(1)}, f32[24,32,2]{1,2,0:T(2,128)S(1)}, f32[24,32,2]{1,2,0:T(2,128)S(1)}, f32...) fusion(f32[24,32]{1,0:T(8,128)S(1)} %copy-done.16, ...), kind=kLoop, calls=%fused_computation.477 | loop fusion | flops 224256 | bytes 1059840 | tf_op jit(solution)/shard_map/add | solution.py:64
  285.6 13.1 %divide_convert_fusion = bf16[24,32,2,64]{1,3,2,0:T(8,128)(2,1)S(1)} fusion(bf16[72,80,2,64]{1,3,2,0:T(8,128)(2,1)S(1)} %bitcast.171, f32[24,32,2]{1,2,0:T(2,128)S(1)} %get-tuple-element.102, f32[24,32,2]{1,2,0:T(2,128)S(1)} %get-tuple-element.151, f32[24,32,2]{1,2,0:T(2,128)S(1)} %get-tuple-element.150, f32[24,32,2]{1,2,0:T(2,128)S(1)} %get-tuple-element.149, ...), kind=kLoop, calls=%fused_computation.4 | loop fusion | flops 14548992 | bytes 10137600 | tf_op jit(solution)/shard_map/convert_element_type | solution.py:69
  298.8 0.5 multiply_reduce_fusion.102
  300.6 0.5 copy-done.5
  301.1 1.0 fusion.24
  (154 shorter events, 7.8 us)
Async XLA Ops:
  4.8 12.6 %collective-permute-start = (bf16[3,32,256]{2,1,0:T(8,128)(2,1)S(1)}, bf16[3,32,256]{2,1,0:T(8,128)(2,1)S(1)}, u32[]{:S(2)}, u32[]{:S(2)}) collective-permute-start(bf16[3,32,256]{2,1,0:T(8,128)(2,1)S(1)} %get-tuple-element.209), channel_id=1, source_target_pairs={{0,4},{4,8},{8,12},{12,16},{16,20},{20,24},{24,28},{28,32},{32,36}... | collective-permute-start | bytes 147464 | tf_op jit(solution)/shard_map/ppermute | solution.py:18
  6.7 10.6 %collective-permute-start.1 = (bf16[3,32,256]{2,1,0:T(8,128)(2,1)S(1)}, bf16[3,32,256]{2,1,0:T(8,128)(2,1)S(1)}, u32[]{:S(2)}, u32[]{:S(2)}) collective-permute-start(bf16[3,32,256]{2,1,0:T(8,128)(2,1)S(1)} %get-tuple-element.210), channel_id=1, source_target_pairs={{4,0},{8,4},{12,8},{16,12},{20,16},{24,20},{28,24},{32,28},{36,32}... | collective-permute-start | bytes 147464 | tf_op jit(solution)/shard_map/ppermute | solution.py:19
  14.4 1.7 copy-start.51
  14.4 1.7 copy-start.52
  17.4 7.6 %collective-permute-start.2 = (bf16[30,3,256]{2,1,0:T(4,128)(2,1)S(1)}, bf16[30,3,256]{2,1,0:T(4,128)(2,1)S(1)}, u32[]{:S(2)}, u32[]{:S(2)}) collective-permute-start(bf16[30,3,256]{2,1,0:T(4,128)(2,1)S(1)} %get-tuple-element.211), channel_id=1, source_target_pairs={{0,1},{1,2},{2,3},{4,5},{5,6},{6,7},{8,9},{9,10},{10,11},{12,13},{... | collective-permute-start | bytes 138248 | tf_op jit(solution)/shard_map/ppermute | solution.py:18
  22.6 9.0 %collective-permute-start.3 = (bf16[30,3,256]{2,1,0:T(4,128)(2,1)S(1)}, bf16[30,3,256]{2,1,0:T(4,128)(2,1)S(1)}, u32[]{:S(2)}, u32[]{:S(2)}) collective-permute-start(bf16[30,3,256]{2,1,0:T(4,128)(2,1)S(1)} %get-tuple-element.212), channel_id=1, source_target_pairs={{1,0},{2,1},{3,2},{5,4},{6,5},{7,6},{9,8},{10,9},{11,10},{13,12},{... | collective-permute-start | bytes 138248 | tf_op jit(solution)/shard_map/ppermute | solution.py:19
  99.7 83.3 %copy-start = (bf16[24,32,128]{2,1,0:T(8,128)(2,1)S(1)}, bf16[24,32,128]{2,1,0:T(8,128)(2,1)}, u32[]{:S(2)}) copy-start(bf16[24,32,128]{2,1,0:T(8,128)(2,1)} %param.8) | copy-start | bytes 589828
  99.7 83.3 %copy-start.6 = (bf16[2,128,128]{2,1,0:T(8,128)(2,1)S(1)}, bf16[2,128,128]{2,1,0:T(8,128)(2,1)}, u32[]{:S(2)}) copy-start(bf16[2,128,128]{2,1,0:T(8,128)(2,1)} %param.12) | copy-start | bytes 196612
  99.7 83.6 %copy-start.50 = (f32[128]{0:T(128)S(1)}, f32[128]{0:T(128)}, u32[]{:S(2)}) copy-start(f32[128]{0:T(128)} %get-tuple-element.312) | copy-start | bytes 1540
  185.1 9.6 %copy-start.53 = (pred[72]{0:T(512)(128)(4,1)S(1)}, pred[72]{0:T(512)(128)(4,1)}, u32[]{:S(2)}) copy-start(pred[72]{0:T(512)(128)(4,1)} %compare_and_fusion.1) | copy-start | bytes 220
  185.1 9.6 %copy-start.54 = (pred[80]{0:T(512)(128)(4,1)S(1)}, pred[80]{0:T(512)(128)(4,1)}, u32[]{:S(2)}) copy-start(pred[80]{0:T(512)(128)(4,1)} %compare_and_fusion) | copy-start | bytes 244
  186.1 12.1 %collective-permute-start.4 = (bf16[24,32,256]{2,1,0:T(8,128)(2,1)S(1)}, bf16[24,32,256]{2,1,0:T(8,128)(2,1)S(1)}, u32[]{:S(2)}, u32[]{:S(2)}) collective-permute-start(bf16[24,32,256]{2,1,0:T(8,128)(2,1)S(1)} %slice.1903), channel_id=1, source_target_pairs={{0,4},{4,8},{8,12},{12,16},{16,20},{20,24},{24,28},{28,32},{32,36}... | collective-permute-start | bytes 1179656 | tf_op jit(solution)/shard_map/ppermute | solution.py:18
  188.0 11.9 %collective-permute-start.5 = (bf16[24,32,256]{2,1,0:T(8,128)(2,1)S(1)}, bf16[24,32,256]{2,1,0:T(8,128)(2,1)S(1)}, u32[]{:S(2)}, u32[]{:S(2)}) collective-permute-start(bf16[24,32,256]{2,1,0:T(8,128)(2,1)S(1)} %slice.1903), channel_id=1, source_target_pairs={{4,0},{8,4},{12,8},{16,12},{20,16},{24,20},{28,24},{32,28},{36,32}... | collective-permute-start | bytes 1179656 | tf_op jit(solution)/shard_map/ppermute | solution.py:19
  201.4 21.9 %collective-permute-start.6 = (bf16[72,24,256]{2,1,0:T(8,128)(2,1)}, bf16[72,24,256]{2,1,0:T(8,128)(2,1)}, u32[]{:S(2)}, u32[]{:S(2)}) collective-permute-start(bf16[72,24,256]{2,1,0:T(8,128)(2,1)} %get-tuple-element.205), channel_id=1, source_target_pairs={{0,1},{1,2},{2,3},{4,5},{5,6},{6,7},{8,9},{9,10},{10,11},{12,13},{... | collective-permute-start | bytes 2654216 | tf_op jit(solution)/shard_map/ppermute | solution.py:18
  208.2 38.5 %collective-permute-start.7 = (bf16[72,24,256]{2,1,0:T(8,128)(2,1)}, bf16[72,24,256]{2,1,0:T(8,128)(2,1)}, u32[]{:S(2)}, u32[]{:S(2)}) collective-permute-start(bf16[72,24,256]{2,1,0:T(8,128)(2,1)} %get-tuple-element.206), channel_id=1, source_target_pairs={{1,0},{2,1},{3,2},{5,4},{6,5},{7,6},{9,8},{10,9},{11,10},{13,12},{... | collective-permute-start | bytes 2654216 | tf_op jit(solution)/shard_map/ppermute | solution.py:19
  280.5 1.5 copy-start.8
  280.5 1.5 copy-start.9
  280.5 1.5 copy-start.10
  280.5 1.5 copy-start.11
  280.5 1.5 copy-start.12
  280.5 1.5 copy-start.13
  280.5 1.5 copy-start.14
  280.6 1.5 copy-start.15
  280.6 1.5 copy-start.16
  280.6 1.5 copy-start.17
  280.6 1.5 copy-start.18
  280.6 1.5 copy-start.19
  280.6 1.5 copy-start.20
  280.6 1.5 copy-start.21
  280.6 1.5 copy-start.22
  280.6 1.5 copy-start.23
  280.6 1.5 copy-start.24
  280.7 1.5 copy-start.25
  280.7 1.5 copy-start.26
  280.7 1.5 copy-start.27
  280.7 1.5 copy-start.28
  280.7 1.5 copy-start.29
  280.7 1.5 copy-start.30
  280.7 1.5 copy-start.31
  280.7 1.5 copy-start.32
  280.7 1.5 copy-start.33
  280.7 1.5 copy-start.34
  280.8 1.5 copy-start.35
  280.8 1.5 copy-start.36
  280.8 1.5 copy-start.37
  280.8 1.5 copy-start.38
  280.8 1.5 copy-start.39
  285.6 13.1 %copy-start.7 = (bf16[2,128,128]{2,1,0:T(8,128)(2,1)S(1)}, bf16[2,128,128]{2,1,0:T(8,128)(2,1)}, u32[]{:S(2)}) copy-start(bf16[2,128,128]{2,1,0:T(8,128)(2,1)} %param.12) | copy-start | bytes 196612
  (15 other events, 18.9 us)
where the time goes:
time: 306 us; the launch traced here: 302 us
  other arithmetic  202 us (66%)
  waiting for transfers between devices  37.7 us (12%)
  starting transfers between devices  32.1 us (10%)
  local copies, waits for them, and re-layouts  24.8 us (8%)
  matrix products  4.58 us (1%)
    convert_element_type x2, other arithmetic, local_window_attend(): return attended.reshape(rows, cols, width).astype(jnp.bfloat16)  96.1 us
    reduce_sum x7, other arithmetic, local_window_attend(): jnp.sum(query_unit * key_part, axis=-1)  72.5 us
    ppermute x4, waiting for transfers between devices, with_halo(): after = lax.ppermute(leading, axis, down)  26.9 us
    add x2, other arithmetic, local_window_attend(): denom = denom + weight  16.7 us
    ppermute x4, starting transfers between devices, with_halo(): after = lax.ppermute(leading, axis, down)  16.2 us
    ppermute x4, starting transfers between devices, with_halo(): before = lax.ppermute(last, axis, up)  15.8 us
    ppermute x4, waiting for transfers between devices, with_halo(): before = lax.ppermute(last, axis, up)  10.8 us
    concatenate x3, other arithmetic, with_halo(): value = jnp.concatenate([before, value, after], axis=dim)  7.9 us
  transfers between devices with their start and end apart: 8, of which 5 were waited for; matrix products, arithmetic and copies ran while one was open for 5% of the time, Pallas kernels for 0%

commit v1 on v0

v1 whole, which is shorter than its diff:
```python
import functools

import jax
import jax.numpy as jnp
import numpy as np
from jax import lax
from jax.experimental import pallas as pl
from jax.experimental.pallas import tpu as pltpu
from jax.sharding import PartitionSpec as P

F32, BF16 = jnp.float32, jnp.bfloat16
MESH = pl.DeviceIdType.MESH
D = 128
FF = 384
ROWS, COLS = 24, 32
STEP = 8
TRIPS = ROWS // STEP
WIDE = 24
CHUNKS = 4
PER = STEP // CHUNKS
TOK = PER * TRIPS * COLS
SIDE = PER * TRIPS * WIDE
BLOCK = TRIPS * (COLS + 2 * WIDE)
LOG2E = 1.4426950408889634


def near_masks():
    a = np.arange(2)[:, None, None, None]
    c = np.arange(COLS)[None, :, None, None]
    kr = np.arange(8)[None, None, :, None]
    rows = (kr - a >= 0) & (kr - a <= 6)
    own = rows & (abs(np.arange(COLS) - c) <= 3)
    slot = np.arange(8)
    side = rows & (abs(np.where(slot < 4, COLS + slot, slot - 8) - c) <= 3)
    return own.reshape(64, 256), side.reshape(64, 64)


def far_mask():
    t = np.arange(TRIPS)[:, None, None]
    c = np.arange(COLS)[None, :, None]
    key_row, key_col = [], []
    for d in range(3):
        for cols in (np.arange(COLS), np.arange(WIDE) - WIDE, np.arange(WIDE) + COLS):
            for t2 in range(TRIPS):
                key_row += [TRIPS * (d - 1) + t2] * len(cols)
                key_col += list(cols)
    key_row, key_col = np.array(key_row), np.array(key_col)
    ok = (abs(key_row - t) <= 3) & ((key_col - c) % STEP == 0) & (abs(key_col - c) <= 3 * STEP)
    return ok.reshape(TRIPS * COLS, 3 * BLOCK)


def dot(a, b):
    return jnp.dot(a, b, preferred_element_type=F32)


def dot_nt(a, b):
    return lax.dot_general(a, b, (((1,), (1,)), ((), ())), preferred_element_type=F32)


def norm(x, gain):
    return x * lax.rsqrt(jnp.mean(x * x, axis=-1, keepdims=True) + 1e-6) * gain


def unit(x, ones):
    return x * lax.rsqrt(dot((x * x).astype(BF16), ones) + 1e-6)


def kernel(
    tok, again, wqkv, sscale, wout, mgain, win, wdown, mown, mside, mfar, out,
    k0, v0, k0s, v0s, q0, x2, upx, dnx, pack_l, pack_r, col_l, col_r,
    h1, hl, hr, rc, lr, k1, v1, s_near, r_near, s_far, r_far,
):
    row, col = lax.axis_index("row"), lax.axis_index("col")
    n_row, n_col = lax.axis_size("row"), lax.axis_size("col")
    up, down = lax.rem(row + n_row - 1, n_row), lax.rem(row + 1, n_row)
    left, right = lax.rem(col + n_col - 1, n_col), lax.rem(col + 1, n_col)

    barrier = pltpu.get_barrier_semaphore()
    around = [
        (down, col), (up, col), (row, right), (row, left),
        (down, right), (up, right), (down, left), (up, left),
    ]
    for device in around:
        pl.semaphore_signal(barrier, inc=1, device_id=device, device_id_type=MESH)

    has_up = (row > 0).astype(F32)
    has_down = (row < n_row - 1).astype(F32)
    has_left = (col > 0).astype(F32)
    has_right = (col < n_col - 1).astype(F32)
    row_ok = (has_up, jnp.float32(1), has_down)

    x0 = tok[...].astype(F32)
    pack_l[...] = x0[:, :8].reshape(ROWS * 8, D).astype(BF16)
    pack_r[...] = x0[:, COLS - 8 :].reshape(ROWS * 8, D).astype(BF16)

    pl.semaphore_wait(barrier, 8)

    def send(src, dst, sems, at, device):
        copy = pltpu.make_async_remote_copy(
            src_ref=src, dst_ref=dst, send_sem=sems[0].at[at], recv_sem=sems[1].at[at],
            device_id=device, device_id_type=MESH,
        )
        copy.start()
        return copy

    edge = ROWS * 8
    near = [
        (pack_r, col_l.at[pl.ds(32, edge)]),
        (pack_l, col_r.at[pl.ds(32, edge)]),
        (tok.at[pl.ds(ROWS - 3, 3)], upx),
        (tok.at[pl.ds(0, 3)], dnx),
        (pack_r.at[pl.ds(edge - 32, 32)], col_l.at[pl.ds(0, 32)]),
        (pack_r.at[pl.ds(0, 32)], col_l.at[pl.ds(edge + 32, 32)]),
        (pack_l.at[pl.ds(edge - 32, 32)], col_r.at[pl.ds(0, 32)]),
        (pack_l.at[pl.ds(0, 32)], col_r.at[pl.ds(edge + 32, 32)]),
    ]
    near_to = [around[i] for i in (2, 3, 0, 1, 4, 5, 6, 7)]
    near_copies = [
        send(src, dst, (s_near, r_near), i, device)
        for i, ((src, dst), device) in enumerate(zip(near, near_to))
    ]

    low = (lax.broadcasted_iota(jnp.int32, (1, D), 1) < D // 2).astype(F32)
    high = 1.0 - low
    same = (lax.broadcasted_iota(jnp.int32, (D, D), 0) < D // 2) == (
        lax.broadcasted_iota(jnp.int32, (D, D), 1) < D // 2
    )
    ones = jnp.where(same, 1.0, 0.0).astype(BF16)

    def query_scale(layer):
        return (sscale[layer, 0] * low + sscale[layer, 1] * high) * LOG2E

    qkv = dot(norm(x0.reshape(ROWS * COLS, D), again[0:1]).astype(BF16), wqkv[0])
    q = unit(qkv[:, :D], ones) * query_scale(0)
    q0[0] = (q * low).astype(BF16)
    q0[1] = (q * high).astype(BF16)
    k0[pl.ds(96, ROWS * COLS)] = unit(qkv[:, D : 2 * D], ones).astype(BF16)
    v0[pl.ds(96, ROWS * COLS), :D] = qkv[:, 2 * D :].astype(BF16)
    v0[pl.ds(96, ROWS * COLS), D:] = jnp.ones((ROWS * COLS, D), BF16)
    v0[pl.ds(0, 96), D:] = jnp.full((96, D), has_up).astype(BF16)
    v0[pl.ds(96 + ROWS * COLS, 96), D:] = jnp.full((96, D), has_down).astype(BF16)
    for d in range(3):
        flags = jnp.concatenate(
            [
                jnp.full((TRIPS * COLS, D), row_ok[d]),
                jnp.full((TRIPS * WIDE, D), row_ok[d] * has_left),
                jnp.full((TRIPS * WIDE, D), row_ok[d] * has_right),
            ],
            axis=0,
        ).astype(BF16)
        for r in range(STEP):
            v1[r, pl.ds(d * BLOCK, BLOCK), D:] = flags

    for copy in near_copies:
        copy.wait_recv()

    slot = lax.broadcasted_iota(jnp.int32, (32, 8, 1), 1)
    side_row = lax.broadcasted_iota(jnp.int32, (32, 8, 1), 0)
    side_x = jnp.where(
        slot < 4,
        col_r[...].astype(F32).reshape(32, 8, D),
        col_l[...].astype(F32).reshape(32, 8, D),
    )
    side_ok = jnp.where(slot < 4, has_right, has_left) * jnp.where(
        side_row < 4, has_up, jnp.where(side_row < 28, 1.0, has_down)
    )
    halo_x = jnp.concatenate(
        [
            upx[...].astype(F32).reshape(96, D),
            dnx[...].astype(F32).reshape(96, D),
            side_x.reshape(256, D)[8:248],
        ],
        axis=0,
    )
    kv = dot(norm(halo_x, again[0:1]).astype(BF16), wqkv[0, :, D:])
    halo_k = unit(kv[:, :D], ones)
    halo_v = kv[:, D:]
    side_ok = jnp.broadcast_to(side_ok.reshape(256, 1)[8:248], (240, D))
    k0[pl.ds(0, 96)] = halo_k[:96].astype(BF16)
    k0[pl.ds(96 + ROWS * COLS, 96)] = halo_k[96:192].astype(BF16)
    k0s[...] = halo_k[192:].astype(BF16)
    v0[pl.ds(0, 96), :D] = (halo_v[:96] * has_up).astype(BF16)
    v0[pl.ds(96 + ROWS * COLS, 96), :D] = (halo_v[96:192] * has_down).astype(BF16)
    v0s[:, :D] = (halo_v[192:] * side_ok).astype(BF16)
    v0s[:, D:] = side_ok.astype(BF16)

    def attend(query, parts):
        size = query.shape[0] // 2
        total = None
        for key, value, mask in parts:
            weight = jnp.exp2(dot_nt(query, key)).astype(BF16)
            weight = weight.reshape(2, size, -1) * mask[None]
            part = dot(weight.reshape(2 * size, -1), value)
            total = part if total is None else total + part
        numer = total[:size, :D] * low + total[size:, :D] * high
        denom = total[:size, D:] * low + total[size:, D:] * high
        return numer / denom

    def finish(x, attended, layer):
        x1 = x + dot(attended.astype(BF16), wout[layer])
        inner = dot(norm(x1, mgain[layer : layer + 1]).astype(BF16), win[layer])
        value, gate = inner[:, :FF], inner[:, FF:]
        half = 0.5 * gate * value
        hidden = half + half * jnp.tanh(
            gate * (0.7978845608028654 + (0.7978845608028654 * 0.044715) * (gate * gate))
        )
        return x1 + dot(hidden.astype(BF16), wdown[layer])

    def near_layer(j):
        attended = []
        for t in range(TRIPS):
            for pair in range(PER // 2):
                i = STEP * t + PER * j + 2 * pair
                result = attend(
                    q0[:, pl.ds(i * COLS, 64)].reshape(128, D),
                    [
                        (k0[pl.ds(i * COLS, 256)], v0[pl.ds(i * COLS, 256)], mown[...]),
                        (k0s[pl.ds(i * 8, 64)], v0s[pl.ds(i * 8, 64)], mside[...]),
                    ],
                )
                attended += [result[:COLS], result[COLS:]]
        order = [(t * PER + r) for r in range(PER) for t in range(TRIPS)]
        attended = jnp.concatenate([attended[i] for i in order], axis=0)
        x = jnp.concatenate(
            [tok[STEP * t + PER * j + r] for r in range(PER) for t in range(TRIPS)], axis=0
        ).astype(F32)
        x = finish(x, attended, 0)
        x2[j] = x
        h = norm(x, again[1:2])
        h1[j] = h.astype(BF16)
        h = h.reshape(PER * TRIPS, COLS, D)
        hl[j] = h[:, :WIDE].reshape(SIDE, D).astype(BF16)
        hr[j] = h[:, COLS - WIDE :].reshape(SIDE, D).astype(BF16)
        sems = (s_far.at[j], r_far.at[j])
        return [
            send(hr.at[j], lr.at[1, j, pl.ds(0, SIDE)], sems, 0, (row, right)),
            send(hl.at[j], lr.at[1, j, pl.ds(SIDE, SIDE)], sems, 1, (row, left)),
            send(h1.at[j], rc.at[0, j], sems, 2, (down, col)),
            send(h1.at[j], rc.at[1, j], sems, 3, (up, col)),
        ]

    def relay(j, copies):
        copies[0].wait_recv()
        copies[1].wait_recv()
        sems = (s_far.at[j], r_far.at[j])
        copies += [
            send(lr.at[1, j], lr.at[0, j], sems, 4, (down, col)),
            send(lr.at[1, j], lr.at[2, j], sems, 5, (up, col)),
        ]

    def far_layer(j, copies):
        own = h1[j]
        q = unit(dot(own, wqkv[1, :, :D]), ones) * query_scale(1)
        for copy in copies[2:]:
            copy.wait_recv()
        for d in range(3):
            centre = own if d == 1 else rc[d // 2, j]
            kv = dot(jnp.concatenate([centre, lr[d, j]], axis=0), wqkv[1, :, D:])
            key, value = unit(kv[:, :D], ones), kv[:, D:]
            value = jnp.concatenate(
                [
                    value[:TOK] * row_ok[d],
                    value[TOK : TOK + SIDE] * (row_ok[d] * has_left),
                    value[TOK + SIDE :] * (row_ok[d] * has_right),
                ],
                axis=0,
            )
            for r in range(PER):
                for array, ref, lanes in ((key, k1, slice(None)), (value, v1, slice(0, D))):
                    piece = jnp.concatenate(
                        [
                            array[r * 96 : (r + 1) * 96],
                            array[TOK + r * 72 : TOK + (r + 1) * 72],
                            array[TOK + SIDE + r * 72 : TOK + SIDE + (r + 1) * 72],
                        ],
                        axis=0,
                    )
                    ref[PER * j + r, pl.ds(d * BLOCK, BLOCK), lanes] = piece.astype(BF16)
        attended = []
        for r in range(PER):
            part = q[r * 96 : (r + 1) * 96]
            query = jnp.concatenate([part * low, part * high], axis=0).astype(BF16)
            attended.append(attend(query, [(k1[PER * j + r], v1[PER * j + r], mfar[...])]))
        x = finish(x2[j], jnp.concatenate(attended, axis=0), 1).astype(BF16)
        for r in range(PER):
            for t in range(TRIPS):
                at = (r * TRIPS + t) * COLS
                out[STEP * t + PER * j + r] = x[at : at + COLS]

    copies = []
    for j in range(CHUNKS):
        copies.append(near_layer(j))
        if j:
            relay(j - 1, copies[j - 1])
    if CHUNKS == 1:
        relay(0, copies[0])
    for j in range(CHUNKS):
        far_layer(j, copies[j])
        if CHUNKS > 1 and j == 0:
            relay(CHUNKS - 1, copies[-1])
    for copy in near_copies + [c for chunk in copies for c in chunk]:
        copy.wait_send()


def shards(tokens, attn_gain, w_qkv, score_scale, w_out, mlp_gain, w_in, down_weight):
    vmem = pl.BlockSpec(memory_space=pltpu.VMEM)
    smem = pl.BlockSpec(memory_space=pltpu.SMEM)
    own, side = near_masks()
    return pl.pallas_call(
        kernel,
        out_shape=jax.ShapeDtypeStruct((ROWS, COLS, D), BF16),
        in_specs=[vmem, vmem, vmem, smem] + [vmem] * 7,
        out_specs=vmem,
        scratch_shapes=[
            pltpu.VMEM((960, D), BF16),
            pltpu.VMEM((960, 2 * D), BF16),
            pltpu.VMEM((240, D), BF16),
            pltpu.VMEM((240, 2 * D), BF16),
            pltpu.VMEM((2, ROWS * COLS, D), BF16),
            pltpu.VMEM((CHUNKS, TOK, D), F32),
            pltpu.VMEM((3, COLS, D), BF16),
            pltpu.VMEM((3, COLS, D), BF16),
            pltpu.VMEM((ROWS * 8, D), BF16),
            pltpu.VMEM((ROWS * 8, D), BF16),
            pltpu.VMEM((256, D), BF16),
            pltpu.VMEM((256, D), BF16),
            pltpu.VMEM((CHUNKS, TOK, D), BF16),
            pltpu.VMEM((CHUNKS, SIDE, D), BF16),
            pltpu.VMEM((CHUNKS, SIDE, D), BF16),
            pltpu.VMEM((2, CHUNKS, TOK, D), BF16),
            pltpu.VMEM((3, CHUNKS, 2 * SIDE, D), BF16),
            pltpu.VMEM((STEP, 3 * BLOCK, D), BF16),
            pltpu.VMEM((STEP, 3 * BLOCK, 2 * D), BF16),
            pltpu.SemaphoreType.DMA((8,)),
            pltpu.SemaphoreType.DMA((8,)),
            pltpu.SemaphoreType.DMA((CHUNKS, 6)),
            pltpu.SemaphoreType.DMA((CHUNKS, 6)),
        ],
        compiler_params=pltpu.CompilerParams(
            collective_id=0, has_side_effects=True, vmem_limit_bytes=40 * 1024 * 1024
        ),
        name="two_layers",
    )(
        tokens, attn_gain, w_qkv, score_scale, w_out, mlp_gain, w_in, down_weight,
        jnp.asarray(own, BF16), jnp.asarray(side, BF16), jnp.asarray(far_mask(), BF16),
    )


def solution(mesh):
    return jax.shard_map(
        shards,
        mesh=mesh,
        in_specs=(P("row", "col", None), P(), P(), P(), P(), P(), P(), P()),
        out_specs=P("row", "col", None),
        check_vma=False,
    )
```

time: 306 us -> 47.2 us (0.15); the launches traced: 302 us -> 46.7 us
  other arithmetic: 202 us -> 0 us
  waiting for transfers between devices: 37.7 us -> 0 us
  Pallas kernels: 0 us -> 37 us
  starting transfers between devices: 32.1 us -> 0 us
  local copies, waits for them, and re-layouts: 24.8 us -> 9.71 us
  matrix products: 4.58 us -> 0 us
    convert_element_type x10 -> x0, other arithmetic: 98.7 us -> none  [the longest x2 96.1 us: local_window_attend(): return attended.reshape(rows, cols, width).astype(jnp.bfloat16)]
    reduce_sum x12 -> x0, other arithmetic: 77.1 us -> none  [the longest x7 72.5 us: local_window_attend(): jnp.sum(query_unit * key_part, axis=-1)]
    ppermute x8 -> x0, waiting for transfers between devices: 37.7 us -> none  [the longest x4 26.9 us: with_halo(): after = lax.ppermute(leading, axis, down)]
    pallas_call x0 -> x1, Pallas kernels: none -> 37 us  [shards(): pl.pallas_call(kernel, out_shape=jax.ShapeDtypeStruct((ROWS, COLS, D), BF...]
    ppermute x8 -> x0, starting transfers between devices: 32.1 us -> none  [the longest x4 16.2 us: with_halo(): after = lax.ppermute(leading, axis, down)]
    add x2 -> x0, other arithmetic: 16.7 us -> none  [local_window_attend(): denom = denom + weight]
    ppermute x2 -> x0, local copies, waits for them, and re-layouts: 9.52 us -> none  [the longest x1 4.82 us: with_halo(): before = lax.ppermute(last, axis, up)]
    unnamed x110 -> x23, local copies, waits for them, and re-layouts: 1.73 us -> 9.71 us
  transfers between devices with their start and end apart: 8 -> 0, of which waited for: 5 -> 0; matrix products, arithmetic and copies ran while one was open for 5% -> 0% of each run, Pallas kernels for 0% -> 0%
where the time goes in v1:
time: 47.2 us; the launch traced here: 46.7 us
  Pallas kernels  37 us (78%)
  local copies, waits for them, and re-layouts  9.71 us (21%)
    pallas_call x1, Pallas kernels, shards(): pl.pallas_call(kernel, out_shape=jax.ShapeDtypeStruct((ROWS, COLS, D), BF...  37 us
    unnamed x23, local copies, waits for them, and re-layouts  9.71 us

profile of v1, /device:TPU:24, one launch (start us, length us, event | category | flops | bytes accessed | tf_op | source)
XLA Modules:
  0.0 46.7 jit_solution(7131537942014690041)
XLA Ops:
  0.0 0.0 copy-start
  0.0 1.0 %copy-done = bf16[2,128,768]{2,1,0:T(8,128)(2,1)S(1)} copy-done((bf16[2,128,768]{2,1,0:T(8,128)(2,1)S(1)}, bf16[2,128,768]{2,1,0:T(8,128)(2,1)}, u32[]{:S(2)}) %copy-start) | copy-done | bytes 393240
  1.0 0.0 copy-start.1
  1.0 0.9 %copy-done.1 = bf16[24,32,128]{2,1,0:T(8,128)(2,1)S(1)} copy-done((bf16[24,32,128]{2,1,0:T(8,128)(2,1)S(1)}, bf16[24,32,128]{2,1,0:T(8,128)(2,1)}, u32[]{:S(2)}) %copy-start.1) | copy-done | bytes 196632
  1.9 0.0 copy-start.2
  1.9 0.9 %copy-done.2 = bf16[2,128,384]{2,1,0:T(8,128)(2,1)S(1)} copy-done((bf16[2,128,384]{2,1,0:T(8,128)(2,1)S(1)}, bf16[2,128,384]{2,1,0:T(8,128)(2,1)}, u32[]{:S(2)}) %copy-start.2) | copy-done | bytes 196632
  2.9 0.0 copy-start.3
  2.9 0.9 %copy-done.3 = bf16[2,384,128]{2,1,0:T(8,128)(2,1)S(1)} copy-done((bf16[2,384,128]{2,1,0:T(8,128)(2,1)S(1)}, bf16[2,384,128]{2,1,0:T(8,128)(2,1)}, u32[]{:S(2)}) %copy-start.3) | copy-done | bytes 196632
  3.8 0.0 copy-start.4
  3.8 0.9 %copy-done.4 = bf16[96,720]{1,0:T(8,128)(2,1)S(1)} copy-done((bf16[96,720]{1,0:T(8,128)(2,1)S(1)}, bf16[96,720]{1,0:T(8,128)(2,1)}, u32[]{:S(2)}) %copy-start.4) | copy-done | bytes 138264
  4.7 0.0 copy-start.5
  4.7 0.8 %copy-done.5 = bf16[2,128,128]{2,1,0:T(8,128)(2,1)S(1)} copy-done((bf16[2,128,128]{2,1,0:T(8,128)(2,1)S(1)}, bf16[2,128,128]{2,1,0:T(8,128)(2,1)}, u32[]{:S(2)}) %copy-start.5) | copy-done | bytes 65560
  5.5 0.0 copy-start.6
  5.5 0.8 %copy-done.6 = bf16[64,256]{1,0:T(8,128)(2,1)S(1)} copy-done((bf16[64,256]{1,0:T(8,128)(2,1)S(1)}, bf16[64,256]{1,0:T(8,128)(2,1)}, u32[]{:S(2)}) %copy-start.6) | copy-done | bytes 32792
  6.3 0.0 copy-start.7
  6.3 0.7 %copy-done.7 = bf16[64,64]{1,0:T(8,128)(2,1)S(1)} copy-done((bf16[64,64]{1,0:T(8,128)(2,1)S(1)}, bf16[64,64]{1,0:T(8,128)(2,1)}, u32[]{:S(2)}) %copy-start.7) | copy-done | bytes 8216
  7.0 0.0 copy-start.8
  7.0 0.7 %copy-done.8 = f32[2,128]{1,0:T(2,128)S(1)} copy-done((f32[2,128]{1,0:T(2,128)S(1)}, f32[2,128]{1,0:T(2,128)}, u32[]{:S(2)}) %copy-start.8) | copy-done | bytes 1048
  7.7 0.0 copy-start.9
  7.7 0.7 %copy-done.9 = f32[2,2]{1,0:T(2,128)S(1)} copy-done((f32[2,2]{1,0:T(2,128)S(1)}, f32[2,2]{1,0:T(2,128)}, u32[]{:S(2)}) %copy-start.9) | copy-done | bytes 40
  8.4 0.0 copy-start.10
  8.4 0.7 %copy-done.10 = f32[2,128]{1,0:T(2,128)S(1)} copy-done((f32[2,128]{1,0:T(2,128)S(1)}, f32[2,128]{1,0:T(2,128)}, u32[]{:S(2)}) %copy-start.10) | copy-done | bytes 1048
  9.0 37.0 %two_layers.1 = bf16[24,32,128]{2,1,0:T(8,128)(2,1)S(1)} custom-call(bf16[24,32,128]{2,1,0:T(8,128)(2,1)S(1)} %copy-done.1, f32[2,128]{1,0:T(2,128)S(1)} %copy-done.8, bf16[2,128,384]{2,1,0:T(8,128)(2,1)S(1)} %copy-done.2, f32[2,2]{1,0:T(2,128)S(1)} %copy-done.9, bf16[2,128,128]{2,1,0:T(8,128)(2,1)S(1)} %copy-done.5, f32[2,128]{1,0:T(2,128)S(1)} %copy-done.10, ...), custom_call_target="tpu_custom_call" | custom-call | tf_op jit(solution)/shard_map/two_layers/pallas_call | solution.py:309
  46.1 0.7 %copy.13 = bf16[24,32,128]{2,1,0:T(8,128)(2,1)} copy(bf16[24,32,128]{2,1,0:T(8,128)(2,1)S(1)} %two_layers.1) | data formatting | bytes 393216
Async XLA Ops:
  0.0 1.0 %copy-start = (bf16[2,128,768]{2,1,0:T(8,128)(2,1)S(1)}, bf16[2,128,768]{2,1,0:T(8,128)(2,1)}, u32[]{:S(2)}) copy-start(bf16[2,128,768]{2,1,0:T(8,128)(2,1)} %win.1) | copy-start | bytes 1179652
  1.0 0.9 %copy-start.1 = (bf16[24,32,128]{2,1,0:T(8,128)(2,1)S(1)}, bf16[24,32,128]{2,1,0:T(8,128)(2,1)}, u32[]{:S(2)}) copy-start(bf16[24,32,128]{2,1,0:T(8,128)(2,1)} %tok.1) | copy-start | bytes 589828
  1.9 0.9 %copy-start.2 = (bf16[2,128,384]{2,1,0:T(8,128)(2,1)S(1)}, bf16[2,128,384]{2,1,0:T(8,128)(2,1)}, u32[]{:S(2)}) copy-start(bf16[2,128,384]{2,1,0:T(8,128)(2,1)} %wqkv.1) | copy-start | bytes 589828
  2.9 0.9 %copy-start.3 = (bf16[2,384,128]{2,1,0:T(8,128)(2,1)S(1)}, bf16[2,384,128]{2,1,0:T(8,128)(2,1)}, u32[]{:S(2)}) copy-start(bf16[2,384,128]{2,1,0:T(8,128)(2,1)} %wdown.1) | copy-start | bytes 589828
  3.8 0.9 %copy-start.4 = (bf16[96,720]{1,0:T(8,128)(2,1)S(1)}, bf16[96,720]{1,0:T(8,128)(2,1)}, u32[]{:S(2)}) copy-start(bf16[96,720]{1,0:T(8,128)(2,1)} %constant.8.clone.mfar) | copy-start | bytes 414724
  4.7 0.8 %copy-start.5 = (bf16[2,128,128]{2,1,0:T(8,128)(2,1)S(1)}, bf16[2,128,128]{2,1,0:T(8,128)(2,1)}, u32[]{:S(2)}) copy-start(bf16[2,128,128]{2,1,0:T(8,128)(2,1)} %wout.1) | copy-start | bytes 196612
  5.5 0.8 %copy-start.6 = (bf16[64,256]{1,0:T(8,128)(2,1)S(1)}, bf16[64,256]{1,0:T(8,128)(2,1)}, u32[]{:S(2)}) copy-start(bf16[64,256]{1,0:T(8,128)(2,1)} %constant.6.clone.mown) | copy-start | bytes 98308
  6.3 0.7 %copy-start.7 = (bf16[64,64]{1,0:T(8,128)(2,1)S(1)}, bf16[64,64]{1,0:T(8,128)(2,1)}, u32[]{:S(2)}) copy-start(bf16[64,64]{1,0:T(8,128)(2,1)} %constant.7.clone.mside) | copy-start | bytes 24580
  7.0 0.7 %copy-start.8 = (f32[2,128]{1,0:T(2,128)S(1)}, f32[2,128]{1,0:T(2,128)}, u32[]{:S(2)}) copy-start(f32[2,128]{1,0:T(2,128)} %again.1) | copy-start | bytes 3076
  7.7 0.7 %copy-start.9 = (f32[2,2]{1,0:T(2,128)S(1)}, f32[2,2]{1,0:T(2,128)}, u32[]{:S(2)}) copy-start(f32[2,2]{1,0:T(2,128)} %sscale.1) | copy-start | bytes 52
  8.4 0.7 %copy-start.10 = (f32[2,128]{1,0:T(2,128)S(1)}, f32[2,128]{1,0:T(2,128)}, u32[]{:S(2)}) copy-start(f32[2,128]{1,0:T(2,128)} %mgain.1) | copy-start | bytes 3076

commit v2 on v1

--- a/solution.py
+++ b/solution.py
@@ -1,8 +1,5 @@
-import functools
-
 import jax
 import jax.numpy as jnp
-import numpy as np
 from jax import lax
 from jax.experimental import pallas as pl
 from jax.experimental.pallas import tpu as pltpu
@@ -24,29 +21,39 @@
 LOG2E = 1.4426950408889634
 
 
+def lanes_and_rows(rows, lanes):
+    at = lax.broadcasted_iota(jnp.int32, (rows, 1), 0)
+    return at >> 5, at & 31, lax.broadcasted_iota(jnp.int32, (1, lanes), 1)
+
+
+def as_mask(ok):
+    return jnp.where(ok, 1.0, 0.0).astype(BF16)
+
+
 def near_masks():
-    a = np.arange(2)[:, None, None, None]
-    c = np.arange(COLS)[None, :, None, None]
-    kr = np.arange(8)[None, None, :, None]
-    rows = (kr - a >= 0) & (kr - a <= 6)
-    own = rows & (abs(np.arange(COLS) - c) <= 3)
-    slot = np.arange(8)
-    side = rows & (abs(np.where(slot < 4, COLS + slot, slot - 8) - c) <= 3)
-    return own.reshape(64, 256), side.reshape(64, 64)
+    a, c, n = lanes_and_rows(64, 256)
+    step = (n >> 5) - a
+    own = (step >= 0) & (step <= 6) & (abs((n & 31) - c) <= 3)
+    a, c, n = lanes_and_rows(64, 64)
+    step, slot = (n >> 3) - a, n & 7
+    side = (step >= 0) & (step <= 6) & (abs(jnp.where(slot < 4, COLS + slot, slot - 8) - c) <= 3)
+    return as_mask(own), as_mask(side)
 
 
 def far_mask():
-    t = np.arange(TRIPS)[:, None, None]
-    c = np.arange(COLS)[None, :, None]
-    key_row, key_col = [], []
-    for d in range(3):
-        for cols in (np.arange(COLS), np.arange(WIDE) - WIDE, np.arange(WIDE) + COLS):
-            for t2 in range(TRIPS):
-                key_row += [TRIPS * (d - 1) + t2] * len(cols)
-                key_col += list(cols)
-    key_row, key_col = np.array(key_row), np.array(key_col)
-    ok = (abs(key_row - t) <= 3) & ((key_col - c) % STEP == 0) & (abs(key_col - c) <= 3 * STEP)
-    return ok.reshape(TRIPS * COLS, 3 * BLOCK)
+    t, c, n = lanes_and_rows(TRIPS * COLS, 3 * BLOCK)
+    d = (n >= BLOCK).astype(jnp.int32) + (n >= 2 * BLOCK).astype(jnp.int32)
+    n = n - BLOCK * d
+    left, right = TRIPS * COLS, TRIPS * (COLS + WIDE)
+    m = jnp.where(n >= right, n - right, n - left)
+    t2 = (m >= WIDE).astype(jnp.int32) + (m >= 2 * WIDE).astype(jnp.int32)
+    m = m - WIDE * t2 + jnp.where(n >= right, COLS, -WIDE)
+    key_col = jnp.where(n < left, n & 31, m)
+    key_row = TRIPS * (d - 1) + jnp.where(n < left, n >> 5, t2)
+    step = key_col - c
+    return as_mask(
+        (abs(key_row - t) <= 3) & ((step & (STEP - 1)) == 0) & (abs(step) <= 3 * STEP)
+    )
 
 
 def dot(a, b):
@@ -65,8 +72,16 @@
     return x * lax.rsqrt(dot((x * x).astype(BF16), ones) + 1e-6)
 
 
-def kernel(
-    tok, again, wqkv, sscale, wout, mgain, win, wdown, mown, mside, mfar, out,
+OPERANDS = 8
+
+
+def kernel(*refs):
+    body(refs[:OPERANDS], *refs[OPERANDS:])
+
+
+def body(
+    given, out,
+    tok, again, wqkv, sscale, wout, mgain, win, wdown, s_given, mown, mside, mfar,
     k0, v0, k0s, v0s, q0, x2, upx, dnx, pack_l, pack_r, col_l, col_r,
     h1, hl, hr, rc, lr, k1, v1, s_near, r_near, s_far, r_far,
 ):
@@ -75,6 +90,14 @@
     up, down = lax.rem(row + n_row - 1, n_row), lax.rem(row + 1, n_row)
     left, right = lax.rem(col + n_col - 1, n_col), lax.rem(col + 1, n_col)
 
+    own = (tok, again, wqkv, sscale, wout, mgain, win, wdown)
+    fetches = [
+        pltpu.make_async_copy(src, dst, s_given.at[i])
+        for i, (src, dst) in enumerate(zip(given, own))
+    ]
+    for fetch in fetches:
+        fetch.start()
+
     barrier = pltpu.get_barrier_semaphore()
     around = [
         (down, col), (up, col), (row, right), (row, left),
@@ -89,6 +112,10 @@
     has_right = (col < n_col - 1).astype(F32)
     row_ok = (has_up, jnp.float32(1), has_down)
 
+    mown[...], mside[...] = near_masks()
+    mfar[...] = far_mask()
+
+    fetches[0].wait()
     x0 = tok[...].astype(F32)
     pack_l[...] = x0[:, :8].reshape(ROWS * 8, D).astype(BF16)
     pack_r[...] = x0[:, COLS - 8 :].reshape(ROWS * 8, D).astype(BF16)
@@ -107,8 +134,8 @@
     near = [
         (pack_r, col_l.at[pl.ds(32, edge)]),
         (pack_l, col_r.at[pl.ds(32, edge)]),
-        (tok.at[pl.ds(ROWS - 3, 3)], upx),
-        (tok.at[pl.ds(0, 3)], dnx),
+        (given[0].at[pl.ds(ROWS - 3, 3)], upx),
+        (given[0].at[pl.ds(0, 3)], dnx),
         (pack_r.at[pl.ds(edge - 32, 32)], col_l.at[pl.ds(0, 32)]),
         (pack_r.at[pl.ds(0, 32)], col_l.at[pl.ds(edge + 32, 32)]),
         (pack_l.at[pl.ds(edge - 32, 32)], col_r.at[pl.ds(0, 32)]),
@@ -128,7 +155,11 @@
     ones = jnp.where(same, 1.0, 0.0).astype(BF16)
 
     def query_scale(layer):
-        return (sscale[layer, 0] * low + sscale[layer, 1] * high) * LOG2E
+        scale = sscale[layer : layer + 1]
+        return (scale[:, :1] * low + scale[:, 1:] * high) * LOG2E
+
+    for fetch in fetches[1:]:
+        fetch.wait()
 
     qkv = dot(norm(x0.reshape(ROWS * COLS, D), again[0:1]).astype(BF16), wqkv[0])
     q = unit(qkv[:, :D], ones) * query_scale(0)
@@ -303,15 +334,18 @@
 
 
 def shards(tokens, attn_gain, w_qkv, score_scale, w_out, mlp_gain, w_in, down_weight):
-    vmem = pl.BlockSpec(memory_space=pltpu.VMEM)
-    smem = pl.BlockSpec(memory_space=pltpu.SMEM)
-    own, side = near_masks()
+    operands = (tokens, attn_gain, w_qkv, score_scale, w_out, mlp_gain, w_in, down_weight)
     return pl.pallas_call(
         kernel,
         out_shape=jax.ShapeDtypeStruct((ROWS, COLS, D), BF16),
-        in_specs=[vmem, vmem, vmem, smem] + [vmem] * 7,
-        out_specs=vmem,
-        scratch_shapes=[
+        in_specs=[pl.BlockSpec(memory_space=pltpu.HBM)] * OPERANDS,
+        out_specs=pl.BlockSpec(memory_space=pltpu.VMEM),
+        scratch_shapes=[pltpu.VMEM(a.shape, a.dtype) for a in operands]
+        + [
+            pltpu.SemaphoreType.DMA((OPERANDS,)),
+            pltpu.VMEM((64, 256), BF16),
+            pltpu.VMEM((64, 64), BF16),
+            pltpu.VMEM((TRIPS * COLS, 3 * BLOCK), BF16),
             pltpu.VMEM((960, D), BF16),
             pltpu.VMEM((960, 2 * D), BF16),
             pltpu.VMEM((240, D), BF16),
@@ -337,13 +371,10 @@
             pltpu.SemaphoreType.DMA((CHUNKS, 6)),
         ],
         compiler_params=pltpu.CompilerParams(
-            collective_id=0, has_side_effects=True, vmem_limit_bytes=40 * 1024 * 1024
+            collective_id=0, has_side_effects=True, vmem_limit_bytes=60 * 1024 * 1024
         ),
         name="two_layers",
-    )(
-        tokens, attn_gain, w_qkv, score_scale, w_out, mlp_gain, w_in, down_weight,
-        jnp.asarray(own, BF16), jnp.asarray(side, BF16), jnp.asarray(far_mask(), BF16),
-    )
+    )(*operands)
 
 
 def solution(mesh):

time: 47.2 us -> 38.9 us (0.82)
  local copies, waits for them, and re-layouts: 9.71 us -> 1.62 us
    unnamed x23 -> x1, local copies, waits for them, and re-layouts: 9.71 us -> 1.62 us
where the time goes in v2:
time: 38.9 us; the launch traced here: 38.7 us
  Pallas kernels  37.1 us (95%)
  local copies, waits for them, and re-layouts  1.62 us (4%)
    pallas_call x1, Pallas kernels, shards(): pl.pallas_call(kernel, out_shape=jax.ShapeDtypeStruct((ROWS, COLS, D), BF...  37.1 us
    unnamed x1, local copies, waits for them, and re-layouts  1.62 us

profile of v2, /device:TPU:24, one launch (start us, length us, event | category | flops | bytes accessed | tf_op | source)
XLA Modules:
  0.0 38.7 jit_solution(7067055982041737254)
XLA Ops:
  0.0 37.1 %two_layers.1 = bf16[24,32,128]{2,1,0:T(8,128)(2,1)} custom-call(bf16[24,32,128]{2,1,0:T(8,128)(2,1)} %refs_0_.1, f32[2,128]{1,0:T(2,128)} %refs_1_.1, bf16[2,128,384]{2,1,0:T(8,128)(2,1)} %refs_2_.1, f32[2,2]{1,0:T(2,128)} %refs_3_.1, bf16[2,128,128]{2,1,0:T(8,128)(2,1)} %refs_4_.1, f32[2,128]{1,0:T(2,128)} %refs_5_.1, bf16[2,128,768]{2,1,0:T(8,128)(2,1)} %refs_6_.1, ...), custom_call_target="tpu_custom_call" | custom-call | tf_op jit(solution)/shard_map/two_layers/pallas_call | solution.py:338
  37.1 1.6 %copy.10 = bf16[24,32,128]{2,1,0:T(8,128)(2,1)} copy(bf16[24,32,128]{2,1,0:T(8,128)(2,1)} %two_layers.1) | data formatting | bytes 393216

commit v3 on v2

v3 whole, which is shorter than its diff:
```python
import jax
import jax.numpy as jnp
from jax import lax
from jax.experimental import pallas as pl
from jax.experimental.pallas import tpu as pltpu
from jax.sharding import PartitionSpec as P

F32, BF16 = jnp.float32, jnp.bfloat16
MESH = pl.DeviceIdType.MESH
D = 128
FF = 384
ROWS, COLS = 24, 32
STEP = 8
TRIPS = ROWS // STEP
WIDE = 24
ROWS_OF = ((3, 11, 19, 4, 12, 20), (9, 17, 10, 18, 1, 2), (5, 13, 6, 14, 21, 22), (7, 15, 8, 16, 23, 0))
BATCHES = (
    (((3, 4), (11, 12), (19, 20)), ((0, 0, 6),)),
    (((9, 10), (17, 18), (5, 6), (13, 14), (7, 8), (15, 16)), ((1, 0, 4), (2, 0, 4), (3, 0, 4))),
    (((1, 2), (21, 22), (23,), (0,)), ((1, 4, 2), (2, 4, 2), (3, 4, 2))),
)
CHUNKS = 4
PER = STEP // CHUNKS
TOK = PER * TRIPS * COLS
SIDE = PER * TRIPS * WIDE
BLOCK = TRIPS * (COLS + 2 * WIDE)
LOG2E = 1.4426950408889634


def lanes_and_rows(rows, lanes):
    at = lax.broadcasted_iota(jnp.int32, (rows, 1), 0)
    return at >> 5, at & 31, lax.broadcasted_iota(jnp.int32, (1, lanes), 1)


def as_mask(ok):
    return jnp.where(ok, 1.0, 0.0).astype(BF16)


def row_mask(first, rows, queries=2):
    a, c, n = lanes_and_rows(queries * COLS, rows * COLS)
    step = (n >> 5) + first - a
    return as_mask((step >= 0) & (step <= 6) & (abs((n & 31) - c) <= 3))


def side_mask(first, queries=2):
    a, c, n = lanes_and_rows(queries * COLS, 64)
    step = 2 * (n >> 4) + ((n >> 2) & 1) + first - a
    at = (n & 3) + jnp.where((n & 8) == 0, -4, COLS)
    return as_mask((step >= 0) & (step <= 6) & (abs(at - c) <= 3))


def far_mask():
    t, c, n = lanes_and_rows(TRIPS * COLS, 3 * BLOCK)
    first = (n >= BLOCK).astype(jnp.int32)
    second = (n >= 2 * BLOCK).astype(jnp.int32)
    n = n - BLOCK * (first + second)
    left, right = TRIPS * COLS, TRIPS * (COLS + WIDE)
    m = jnp.where(n >= right, n - right, n - left)
    t2 = (m >= WIDE).astype(jnp.int32) + (m >= 2 * WIDE).astype(jnp.int32)
    m = m - WIDE * t2 + jnp.where(n >= right, COLS, -WIDE)
    key_col = jnp.where(n < left, n & 31, m)
    key_row = TRIPS * (2 * second - first) + jnp.where(n < left, n >> 5, t2)
    step = key_col - c
    return as_mask(
        (abs(key_row - t) <= 3) & ((step & (STEP - 1)) == 0) & (abs(step) <= 3 * STEP)
    )


def dot(a, b):
    return jnp.dot(a, b, preferred_element_type=F32)


def dot_nt(a, b):
    return lax.dot_general(a, b, (((1,), (1,)), ((), ())), preferred_element_type=F32)


def norm(x, gain):
    return x * lax.rsqrt(jnp.mean(x * x, axis=-1, keepdims=True) + 1e-6) * gain


def unit(x, ones):
    return x * lax.rsqrt(dot((x * x).astype(BF16), ones) + 1e-6)


OPERANDS = 8


def kernel(*refs):
    body(refs[:OPERANDS], *refs[OPERANDS:])


def body(
    given, out,
    tok, again, wqkv, sscale, wout, mgain, win, wdown, s_given, mown, mside, mfar,
    k0, v0, k0e, v0e, k0s, v0s, q0, acc0, x2, upx, dnx, pack_l, pack_r, beside,
    h1, hl, hr, rc, lr, q1, k1, v1, acc1, s_near, r_near, s_far, r_far,
):
    row, col = lax.axis_index("row"), lax.axis_index("col")
    n_row, n_col = lax.axis_size("row"), lax.axis_size("col")
    up, down = lax.rem(row + n_row - 1, n_row), lax.rem(row + 1, n_row)
    left, right = lax.rem(col + n_col - 1, n_col), lax.rem(col + 1, n_col)

    own = (tok, again, wqkv, sscale, wout, mgain, win, wdown)
    fetches = [
        pltpu.make_async_copy(src, dst, s_given.at[i])
        for i, (src, dst) in enumerate(zip(given, own))
    ]
    for fetch in fetches:
        fetch.start()

    barrier = pltpu.get_barrier_semaphore()
    around = [(down, col), (up, col), (row, right), (row, left)]
    for device in around:
        pl.semaphore_signal(barrier, inc=1, device_id=device, device_id_type=MESH)

    has_up = (row > 0).astype(F32)
    has_down = (row < n_row - 1).astype(F32)
    has_left = (col > 0).astype(F32)
    has_right = (col < n_col - 1).astype(F32)
    row_ok = (jnp.float32(1), has_up, has_down)

    mown[...] = row_mask(0, 8)
    mside[...] = side_mask(0)
    mfar[...] = far_mask()

    fetches[0].wait()
    x0 = tok[...].astype(F32)
    even, odd = (x0.reshape(ROWS // 2, 2, COLS, D)[:, i] for i in range(2))
    slot = lax.broadcasted_iota(jnp.int32, (1, 8, 1), 1) < 4
    pack_l[...] = (
        jnp.where(slot, even[:, :8], pltpu.roll(odd[:, :8], 4, 1)).reshape(96, D).astype(BF16)
    )
    pack_r[...] = (
        jnp.where(slot, pltpu.roll(even[:, COLS - 8 :], 4, 1), odd[:, COLS - 8 :])
        .reshape(96, D)
        .astype(BF16)
    )

    def send(src, dst, sems, at, device):
        copy = pltpu.make_async_remote_copy(
            src_ref=src, dst_ref=dst, send_sem=sems[0].at[at], recv_sem=sems[1].at[at],
            device_id=device, device_id_type=MESH,
        )
        copy.start()
        return copy

    lane = lax.broadcasted_iota(jnp.int32, (1, 2 * D), 1)
    first_head = (lane & (D // 2)) == 0
    low = jnp.where(first_head[:, :D], 1.0, 0.0)
    high = 1.0 - low
    same = (lax.broadcasted_iota(jnp.int32, (D, D), 0) < D // 2) == (
        lax.broadcasted_iota(jnp.int32, (D, D), 1) < D // 2
    )
    ones = jnp.where(same, 1.0, 0.0).astype(BF16)

    def query_scale(layer):
        scale = sscale[layer : layer + 1]
        return (scale[:, :1] * low + scale[:, 1:] * high) * LOG2E

    for fetch in fetches[1:]:
        fetch.wait()

    def attend(query, parts):
        size = query.shape[0] // 2
        total = None
        for key, value, mask in parts:
            weight = jnp.exp2(dot_nt(query, key)).astype(BF16)
            weight = weight.reshape(2, size, -1) * mask[None]
            part = dot(weight.reshape(2 * size, -1), value)
            total = part if total is None else total + part
        return jnp.where(first_head, total[:size], total[size:])

    qkv = dot(norm(x0.reshape(ROWS * COLS, D), again[0:1]).astype(BF16), wqkv[0])
    q = unit(qkv[:, :D], ones) * query_scale(0)
    q0[0] = (q * low).astype(BF16)
    q0[1] = (q * high).astype(BF16)
    k0[...] = unit(qkv[:, D : 2 * D], ones).astype(BF16)
    v0[:, :D] = qkv[:, 2 * D :].astype(BF16)
    v0[:, D:] = jnp.ones((ROWS * COLS, D), BF16)

    pl.semaphore_wait(barrier, 4)
    near = (s_near, r_near)
    near_copies = [
        send(pack_r, beside.at[0, pl.ds(16, 96)], near, 0, (row, right)),
        send(pack_l, beside.at[1, pl.ds(16, 96)], near, 1, (row, left)),
        send(given[0].at[pl.ds(ROWS - 3, 3)], upx, near, 2, (down, col)),
        send(given[0].at[pl.ds(0, 3)], dnx, near, 3, (up, col)),
    ]

    def query_of(rows):
        size = len(rows) * COLS
        return q0[:, pl.ds(rows[0] * COLS, size)].reshape(2 * size, D)

    for groups, _ in BATCHES:
        for rows in groups:
            i, end = rows[0], min(rows[-1] + 4, ROWS)
            begin = max(i - 3, 0)
            keys = pl.ds(begin * COLS, (end - begin) * COLS)
            whole = end - begin == 8
            mask = mown[...] if whole else row_mask(begin - i + 3, end - begin, len(rows))
            acc0[pl.ds(i * COLS, len(rows) * COLS)] = attend(
                query_of(rows), [(k0[keys], v0[keys], mask)]
            )
    v0e[pl.ds(0, 96), D:] = jnp.full((96, D), has_up).astype(BF16)
    v0e[pl.ds(96, 96), D:] = jnp.full((96, D), has_down).astype(BF16)
    for d in range(3):
        flags = jnp.concatenate(
            [
                jnp.full((TRIPS * COLS, D), row_ok[d]),
                jnp.full((TRIPS * WIDE, D), row_ok[d] * has_left),
                jnp.full((TRIPS * WIDE, D), row_ok[d] * has_right),
            ],
            axis=0,
        ).astype(BF16)
        for r in range(STEP):
            v1[r, pl.ds(d * BLOCK, BLOCK), D:] = flags

    def halo_keys(x):
        kv = dot(norm(x, again[0:1]).astype(BF16), wqkv[0, :, D:])
        return unit(kv[:, :D], ones).astype(BF16), kv[:, D:]

    def side_tokens(at, size):
        both = [beside[i, pl.ds(at, size)].astype(F32).reshape(size // 8, 8, D) for i in range(2)]
        return jnp.stack(both, axis=1).reshape(2 * size, D)

    def side_ok(size, flag):
        at = lax.broadcasted_iota(jnp.int32, (size, D), 0)
        return jnp.where((at & 8) == 0, has_left, has_right) * flag

    for copy in near_copies[:2]:
        copy.wait_recv()
    near_copies += [
        send(beside.at[:, pl.ds(96, 16)], beside.at[:, pl.ds(0, 16)], near, 4, (down, col)),
        send(beside.at[:, pl.ds(16, 16)], beside.at[:, pl.ds(112, 16)], near, 5, (up, col)),
    ]
    key, value = halo_keys(side_tokens(16, 96))
    k0s[pl.ds(32, 192)] = key
    ok = side_ok(192, 1.0)
    v0s[pl.ds(32, 192), :D] = (value * ok).astype(BF16)
    v0s[pl.ds(32, 192), D:] = ok.astype(BF16)

    def far_halo():
        for copy in near_copies[2:]:
            copy.wait_recv()
        x = jnp.concatenate(
            [
                upx[...].astype(F32).reshape(96, D),
                dnx[...].astype(F32).reshape(96, D),
                side_tokens(0, 16),
                side_tokens(112, 16),
            ],
            axis=0,
        )
        key, value = halo_keys(x)
        k0e[...] = key[:192]
        v0e[pl.ds(0, 96), :D] = (value[:96] * has_up).astype(BF16)
        v0e[pl.ds(96, 96), :D] = (value[96:192] * has_down).astype(BF16)
        for at, place, flag in ((192, 0, has_up), (224, 224, has_down)):
            ok = side_ok(32, flag)
            k0s[pl.ds(place, 32)] = key[at : at + 32]
            v0s[pl.ds(place, 32), :D] = (value[at : at + 32] * ok).astype(BF16)
            v0s[pl.ds(place, 32), D:] = ok.astype(BF16)

    def finish(x, attended, layer):
        x1 = x + dot(attended.astype(BF16), wout[layer])
        inner = dot(norm(x1, mgain[layer : layer + 1]).astype(BF16), win[layer])
        value, gate = inner[:, :FF], inner[:, FF:]
        half = 0.5 * gate * value
        hidden = half + half * jnp.tanh(
            gate * (0.7978845608028654 + (0.7978845608028654 * 0.044715) * (gate * gate))
        )
        return x1 + dot(hidden.astype(BF16), wdown[layer])

    sides = [[] for _ in range(CHUNKS)]
    centres = [[] for _ in range(CHUNKS)]
    relays = [[] for _ in range(CHUNKS)]

    def near_layer(groups, pieces):
        attended = {}
        for rows in groups:
            i = rows[0]
            first = 2 * ((i + 1) // 2) - 4
            keys = pl.ds((i + 1) // 2 * 16, 64)
            whole = len(rows) == 2
            mask = mside[...] if whole else side_mask(first - i + 3, 1)
            parts = [(k0s[keys], v0s[keys], mask)]
            if i < 3:
                parts.append((k0e[pl.ds(0, 96)], v0e[pl.ds(0, 96)], row_mask(-i, 3, len(rows))))
            if rows[-1] + 4 > ROWS:
                mask = row_mask(ROWS + 3 - i, 3, len(rows))
                parts.append((k0e[pl.ds(96, 96)], v0e[pl.ds(96, 96)], mask))
            result = acc0[pl.ds(i * COLS, len(rows) * COLS)] + attend(query_of(rows), parts)
            result = result[:, :D] / result[:, D:]
            for at, one in enumerate(rows):
                attended[one] = result[at * COLS : (at + 1) * COLS]
        order = [ROWS_OF[j][p] for j, start, size in pieces for p in range(start, start + size)]
        x = jnp.concatenate([tok[i] for i in order], axis=0).astype(F32)
        x = finish(x, jnp.concatenate([attended[i] for i in order], axis=0), 0)
        h = norm(x, again[1:2])
        at = 0
        for j, start, size in pieces:
            whole = pl.ds(start * COLS, size * COLS)
            part = pl.ds(start * WIDE, size * WIDE)
            rows = slice(at, at + size * COLS)
            at += size * COLS
            piece = h[rows].reshape(size, COLS, D)
            hl[j, part] = piece[:, :WIDE].reshape(size * WIDE, D).astype(BF16)
            hr[j, part] = piece[:, COLS - WIDE :].reshape(size * WIDE, D).astype(BF16)
            h1[j, whole] = h[rows].astype(BF16)
            x2[j, whole] = x[rows]
        for j, start, size in pieces:
            part = pl.ds(start * WIDE, size * WIDE)
            other = pl.ds(SIDE + start * WIDE, size * WIDE)
            sems = (s_far.at[j], r_far.at[j])
            k = 0 if start == 0 else 2
            sides[j] += [
                send(hr.at[j, part], lr.at[0, j, part], sems, k, (row, right)),
                send(hl.at[j, part], lr.at[0, j, other], sems, k + 1, (row, left)),
            ]
        for j, start, size in pieces:
            whole = pl.ds(start * COLS, size * COLS)
            sems = (s_far.at[j], r_far.at[j])
            k = 4 if start == 0 else 6
            centres[j] += [
                send(h1.at[j, whole], rc.at[0, j, whole], sems, k, (down, col)),
                send(h1.at[j, whole], rc.at[1, j, whole], sems, k + 1, (up, col)),
            ]

    def relay(j):
        for copy in sides[j]:
            copy.wait_recv()
        sems = (s_far.at[j], r_far.at[j])
        relays[j] += [
            send(lr.at[0, j], lr.at[1, j], sems, 8, (down, col)),
            send(lr.at[0, j], lr.at[2, j], sems, 9, (up, col)),
        ]

    def residues(j):
        firsts = sorted({i % STEP for i in ROWS_OF[j]})
        return [[ROWS_OF[j].index(i + STEP * t) for t in range(TRIPS)] for i in firsts]

    def far_keys(j, d):
        centre = h1[j] if d == 0 else rc[d - 1, j]
        kv = dot(jnp.concatenate([centre, lr[d, j]], axis=0), wqkv[1, :, D:])
        key, value = unit(kv[:, :D], ones), kv[:, D:]
        value = jnp.concatenate(
            [
                value[:TOK] * row_ok[d],
                value[TOK : TOK + SIDE] * (row_ok[d] * has_left),
                value[TOK + SIDE :] * (row_ok[d] * has_right),
            ],
            axis=0,
        )
        for r, places in enumerate(residues(j)):
            for array, ref, lanes in ((key, k1, slice(None)), (value, v1, slice(0, D))):
                piece = jnp.concatenate(
                    [array[p * COLS : (p + 1) * COLS] for p in places]
                    + [
                        array[base + p * WIDE : base + (p + 1) * WIDE]
                        for base in (TOK, TOK + SIDE)
                        for p in places
                    ],
                    axis=0,
                )
                ref[PER * j + r, pl.ds(d * BLOCK, BLOCK), lanes] = piece.astype(BF16)

    def far_own(j):
        q = unit(dot(h1[j], wqkv[1, :, :D]), ones) * query_scale(1)
        far_keys(j, 0)
        for r, places in enumerate(residues(j)):
            part = jnp.concatenate([q[p * COLS : (p + 1) * COLS] for p in places], axis=0)
            query = jnp.concatenate([part * low, part * high], axis=0).astype(BF16)
            q1[PER * j + r] = query
            keys = (PER * j + r, pl.ds(0, BLOCK))
            acc1[PER * j + r] = attend(query, [(k1[keys], v1[keys], mfar[:, :BLOCK])])

    def far_layer(j):
        for copy in centres[j] + relays[j]:
            copy.wait_recv()
        far_keys(j, 1)
        far_keys(j, 2)
        attended = [None] * len(ROWS_OF[j])
        for r, places in enumerate(residues(j)):
            keys = (PER * j + r, pl.ds(BLOCK, 2 * BLOCK))
            result = acc1[PER * j + r] + attend(
                q1[PER * j + r], [(k1[keys], v1[keys], mfar[:, BLOCK:])]
            )
            result = result[:, :D] / result[:, D:]
            for t, p in enumerate(places):
                attended[p] = result[t * COLS : (t + 1) * COLS]
        x = finish(x2[j], jnp.concatenate(attended, axis=0), 1).astype(BF16)
        for p, i in enumerate(ROWS_OF[j]):
            out[i] = x[p * COLS : (p + 1) * COLS]

    near_layer(*BATCHES[0])
    near_layer(*BATCHES[1])
    far_halo()
    near_layer(*BATCHES[2])
    for j in range(CHUNKS):
        relay(j)
        far_own(j)
    for j in range(CHUNKS):
        far_layer(j)
    for copy in near_copies + sum(sides + centres + relays, []):
        copy.wait_send()


def shards(tokens, attn_gain, w_qkv, score_scale, w_out, mlp_gain, w_in, down_weight):
    operands = (tokens, attn_gain, w_qkv, score_scale, w_out, mlp_gain, w_in, down_weight)
    operands = [pltpu.with_memory_space_constraint(a, pltpu.HBM) for a in operands]
    return pl.pallas_call(
        kernel,
        out_shape=jax.ShapeDtypeStruct((ROWS, COLS, D), BF16),
        in_specs=[pl.BlockSpec(memory_space=pltpu.HBM)] * OPERANDS,
        out_specs=pl.BlockSpec(memory_space=pltpu.VMEM),
        scratch_shapes=[pltpu.VMEM(a.shape, a.dtype) for a in operands]
        + [
            pltpu.SemaphoreType.DMA((OPERANDS,)),
            pltpu.VMEM((64, 256), BF16),
            pltpu.VMEM((64, 64), BF16),
            pltpu.VMEM((TRIPS * COLS, 3 * BLOCK), BF16),
            pltpu.VMEM((ROWS * COLS, D), BF16),
            pltpu.VMEM((ROWS * COLS, 2 * D), BF16),
            pltpu.VMEM((192, D), BF16),
            pltpu.VMEM((192, 2 * D), BF16),
            pltpu.VMEM((256, D), BF16),
            pltpu.VMEM((256, 2 * D), BF16),
            pltpu.VMEM((2, ROWS * COLS, D), BF16),
            pltpu.VMEM((ROWS * COLS, 2 * D), F32),
            pltpu.VMEM((CHUNKS, TOK, D), F32),
            pltpu.VMEM((3, COLS, D), BF16),
            pltpu.VMEM((3, COLS, D), BF16),
            pltpu.VMEM((96, D), BF16),
            pltpu.VMEM((96, D), BF16),
            pltpu.VMEM((2, 128, D), BF16),
            pltpu.VMEM((CHUNKS, TOK, D), BF16),
            pltpu.VMEM((CHUNKS, SIDE, D), BF16),
            pltpu.VMEM((CHUNKS, SIDE, D), BF16),
            pltpu.VMEM((2, CHUNKS, TOK, D), BF16),
            pltpu.VMEM((3, CHUNKS, 2 * SIDE, D), BF16),
            pltpu.VMEM((STEP, 2 * TRIPS * COLS, D), BF16),
            pltpu.VMEM((STEP, 3 * BLOCK, D), BF16),
            pltpu.VMEM((STEP, 3 * BLOCK, 2 * D), BF16),
            pltpu.VMEM((STEP, TRIPS * COLS, 2 * D), F32),
            pltpu.SemaphoreType.DMA((6,)),
            pltpu.SemaphoreType.DMA((6,)),
            pltpu.SemaphoreType.DMA((CHUNKS, 10)),
            pltpu.SemaphoreType.DMA((CHUNKS, 10)),
        ],
        compiler_params=pltpu.CompilerParams(
            collective_id=0, has_side_effects=True, vmem_limit_bytes=48 * 1024 * 1024
        ),
        name="two_layers",
    )(*operands)


def solution(mesh):
    return jax.shard_map(
        shards,
        mesh=mesh,
        in_specs=(P("row", "col", None), P(), P(), P(), P(), P(), P(), P()),
        out_specs=P("row", "col", None),
        check_vma=False,
    )
```

time: 38.9 us -> 33.2 us (0.85)
  the two profiles are of different devices: /device:TPU:24 before, /device:TPU:64 now
where the time goes in v3:
time: 33.2 us; the launch traced here: 33.1 us
  Pallas kernels  32.4 us (98%)
  local copies, waits for them, and re-layouts  0.68 us (2%)
    pallas_call x1, Pallas kernels, shards(): pl.pallas_call(kernel, out_shape=jax.ShapeDtypeStruct((ROWS, COLS, D), BF...  32.4 us
    unnamed x1, local copies, waits for them, and re-layouts  0.68 us

profile of v3, /device:TPU:64, one launch (start us, length us, event | category | flops | bytes accessed | tf_op | source)
XLA Modules:
  0.0 33.1 jit_solution(6178009918872863639)
XLA Ops:
  0.0 32.4 %two_layers.1 = bf16[24,32,128]{2,1,0:T(8,128)(2,1)S(1)} custom-call(bf16[24,32,128]{2,1,0:T(8,128)(2,1)} %refs_0_.1, f32[2,128]{1,0:T(2,128)} %refs_1_.1, bf16[2,128,384]{2,1,0:T(8,128)(2,1)} %refs_2_.1, f32[2,2]{1,0:T(2,128)} %refs_3_.1, bf16[2,128,128]{2,1,0:T(8,128)(2,1)} %refs_4_.1, f32[2,128]{1,0:T(2,128)} %refs_5_.1, bf16[2,128,768]{2,1,0:T(8,128)(2,1)} %refs_6_.1, ...), custom_call_target="tpu_custom_call" | custom-call | tf_op jit(solution)/shard_map/two_layers/pallas_call | solution.py:411
  32.4 0.7 %copy.10 = bf16[24,32,128]{2,1,0:T(8,128)(2,1)} copy(bf16[24,32,128]{2,1,0:T(8,128)(2,1)S(1)} %two_layers.1) | data formatting | bytes 393216

commit v4 on v3

v4 whole, which is shorter than its diff:
```python
import jax
import jax.numpy as jnp
from jax import lax
from jax.experimental import pallas as pl
from jax.experimental.pallas import tpu as pltpu
from jax.sharding import PartitionSpec as P

F32, BF16 = jnp.float32, jnp.bfloat16
MESH = pl.DeviceIdType.MESH
D = 128
FF = 384
ROWS, COLS = 24, 32
STEP = 8
TRIPS = ROWS // STEP
WIDE = 24
ROWS_OF = ((3, 11, 19, 4, 12, 20), (9, 17, 10, 18, 1, 2), (5, 13, 6, 14, 21, 22), (7, 15, 8, 16, 23, 0))
EDGE = (0, 1, 2, 21, 22, 23)
GROUPS = ((3, 4), (11, 12), (19, 20), (9, 10), (17, 18), (5, 6), (13, 14), (7, 8), (15, 16))
EDGE_GROUPS = ((1, 2), (21, 22), (23,), (0,))
CHUNKS = 4
PER = STEP // CHUNKS
TOK = PER * TRIPS * COLS
SIDE = PER * TRIPS * WIDE
BLOCK = TRIPS * (COLS + 2 * WIDE)
LOG2E = 1.4426950408889634


def pieces_of(j):
    inner = [i for i in ROWS_OF[j] if i not in EDGE]
    outer = [i for i in ROWS_OF[j] if i in EDGE]
    return [(0, inner)] + ([(len(inner), outer)] if outer else [])


def segments(rows):
    return [[(i, a, b) for i in rows] for a, b in ((24, 32), (8, 24), (0, 8))]


def place_in(j, segs, per_row):
    found = {}
    for first, rows in pieces_of(j):
        at = first * per_row
        for seg in segs:
            a, b = seg
            for i in rows:
                found[i, a] = at
                at += b - a
    return found


def lanes_and_rows(rows, lanes):
    at = lax.broadcasted_iota(jnp.int32, (rows, 1), 0)
    return at >> 5, at & 31, lax.broadcasted_iota(jnp.int32, (1, lanes), 1)


def as_mask(ok):
    return jnp.where(ok, 1.0, 0.0).astype(BF16)


def row_mask(first, rows, queries=2):
    a, c, n = lanes_and_rows(queries * COLS, rows * COLS)
    step = (n >> 5) + first - a
    return as_mask((step >= 0) & (step <= 6) & (abs((n & 31) - c) <= 3))


def side_mask(first, queries=2):
    a, c, n = lanes_and_rows(queries * COLS, 64)
    step = 2 * (n >> 4) + ((n >> 2) & 1) + first - a
    at = (n & 3) + jnp.where((n & 8) == 0, -4, COLS)
    return as_mask((step >= 0) & (step <= 6) & (abs(at - c) <= 3))


def far_mask():
    t, c, n = lanes_and_rows(TRIPS * COLS, 3 * BLOCK)
    first = (n >= BLOCK).astype(jnp.int32)
    second = (n >= 2 * BLOCK).astype(jnp.int32)
    n = n - BLOCK * (first + second)
    left, right = TRIPS * COLS, TRIPS * (COLS + WIDE)
    m = jnp.where(n >= right, n - right, n - left)
    t2 = (m >= WIDE).astype(jnp.int32) + (m >= 2 * WIDE).astype(jnp.int32)
    m = m - WIDE * t2 + jnp.where(n >= right, COLS, -WIDE)
    key_col = jnp.where(n < left, n & 31, m)
    key_row = TRIPS * (2 * second - first) + jnp.where(n < left, n >> 5, t2)
    step = key_col - c
    return as_mask(
        (abs(key_row - t) <= 3) & ((step & (STEP - 1)) == 0) & (abs(step) <= 3 * STEP)
    )


def dot(a, b):
    return jnp.dot(a, b, preferred_element_type=F32)


def dot_nt(a, b):
    return lax.dot_general(a, b, (((1,), (1,)), ((), ())), preferred_element_type=F32)


def norm(x, gain):
    return x * lax.rsqrt(jnp.mean(x * x, axis=-1, keepdims=True) + 1e-6) * gain


def unit(x, ones):
    return x * lax.rsqrt(dot((x * x).astype(BF16), ones) + 1e-6)


OPERANDS = 8


def kernel(*refs):
    body(refs[:OPERANDS], *refs[OPERANDS:])


def body(
    given, out,
    tok, again, wqkv, sscale, wout, mgain, win, wdown, s_given, mown, mside, mfar,
    k0, v0, k0e, v0e, k0s, v0s, q0, acc0, x2, upx, dnx, pack_l, pack_r, beside,
    h1, rc, lr, q1, k1, v1, acc1, s_near, r_near, s_far, r_far,
):
    row, col = lax.axis_index("row"), lax.axis_index("col")
    n_row, n_col = lax.axis_size("row"), lax.axis_size("col")
    up, down = lax.rem(row + n_row - 1, n_row), lax.rem(row + 1, n_row)
    left, right = lax.rem(col + n_col - 1, n_col), lax.rem(col + 1, n_col)

    own = (tok, again, wqkv, sscale, wout, mgain, win, wdown)
    fetches = [
        pltpu.make_async_copy(src, dst, s_given.at[i])
        for i, (src, dst) in enumerate(zip(given, own))
    ]
    for fetch in fetches:
        fetch.start()

    barrier = pltpu.get_barrier_semaphore()
    exists = {"up": row > 0, "down": row < n_row - 1, "left": col > 0, "right": col < n_col - 1}
    device_at = {"up": (up, col), "down": (down, col), "left": (row, left), "right": (row, right)}
    opposite = {"up": "down", "down": "up", "left": "right", "right": "left"}

    absent = {
        "up": (upx, beside.at[:, pl.ds(0, 16)], rc.at[0], lr.at[1]),
        "down": (dnx, beside.at[:, pl.ds(112, 16)], rc.at[1], lr.at[2]),
        "left": (beside.at[0, pl.ds(16, 96)], lr.at[0, :, 0]),
        "right": (beside.at[1, pl.ds(16, 96)], lr.at[0, :, 1]),
    }
    for way, refs in absent.items():

        @pl.when(jnp.logical_not(exists[way]))
        def _(refs=refs):
            for ref in refs:
                ref[...] = jnp.zeros(ref.shape, ref.dtype)

    for way, device in device_at.items():

        @pl.when(exists[way])
        def _(device=device):
            pl.semaphore_signal(barrier, inc=1, device_id=device, device_id_type=MESH)

    has_up, has_down, has_left, has_right = (exists[way].astype(F32) for way in device_at)
    greeted = sum(exists[way].astype(jnp.int32) for way in device_at)
    row_ok = (jnp.float32(1), has_up, has_down)

    mown[...] = row_mask(0, 8)
    mside[...] = side_mask(0)
    mfar[...] = far_mask()

    fetches[0].wait()
    x0 = tok[...].astype(F32)
    even, odd = (x0.reshape(ROWS // 2, 2, COLS, D)[:, i] for i in range(2))
    slot = lax.broadcasted_iota(jnp.int32, (1, 8, 1), 1) < 4
    pack_l[...] = (
        jnp.where(slot, even[:, :8], pltpu.roll(odd[:, :8], 4, 1)).reshape(96, D).astype(BF16)
    )
    pack_r[...] = (
        jnp.where(slot, pltpu.roll(even[:, COLS - 8 :], 4, 1), odd[:, COLS - 8 :])
        .reshape(96, D)
        .astype(BF16)
    )

    class Message:
        def __init__(self, src, dst, sems, at, way):
            self.copy = pltpu.make_async_remote_copy(
                src_ref=src, dst_ref=dst, send_sem=sems[0].at[at], recv_sem=sems[1].at[at],
                device_id=device_at[way], device_id_type=MESH,
            )
            self.sends, self.receives = exists[way], exists[opposite[way]]
            pl.when(self.sends)(self.copy.start)

        def wait_recv(self):
            pl.when(self.receives)(self.copy.wait_recv)

        def wait_send(self):
            pl.when(self.sends)(self.copy.wait_send)

    send = Message

    lane = lax.broadcasted_iota(jnp.int32, (1, 2 * D), 1)
    first_head = (lane & (D // 2)) == 0
    low = jnp.where(first_head[:, :D], 1.0, 0.0)
    high = 1.0 - low
    same = (lax.broadcasted_iota(jnp.int32, (D, D), 0) < D // 2) == (
        lax.broadcasted_iota(jnp.int32, (D, D), 1) < D // 2
    )
    ones = jnp.where(same, 1.0, 0.0).astype(BF16)

    def query_scale(layer):
        scale = sscale[layer : layer + 1]
        return (scale[:, :1] * low + scale[:, 1:] * high) * LOG2E

    for fetch in fetches[1:]:
        fetch.wait()

    def attend(query, parts):
        size = query.shape[0] // 2
        total = None
        for key, value, mask in parts:
            weight = jnp.exp2(dot_nt(query, key)).astype(BF16)
            weight = weight.reshape(2, size, -1) * mask[None]
            part = dot(weight.reshape(2 * size, -1), value)
            total = part if total is None else total + part
        return jnp.where(first_head, total[:size], total[size:])

    qkv = dot(norm(x0.reshape(ROWS * COLS, D), again[0:1]).astype(BF16), wqkv[0])
    q = unit(qkv[:, :D], ones) * query_scale(0)
    q0[0] = (q * low).astype(BF16)
    q0[1] = (q * high).astype(BF16)
    k0[...] = unit(qkv[:, D : 2 * D], ones).astype(BF16)
    v0[:, :D] = qkv[:, 2 * D :].astype(BF16)
    v0[:, D:] = jnp.ones((ROWS * COLS, D), BF16)

    pl.semaphore_wait(barrier, greeted)
    near = (s_near, r_near)
    near_copies = [
        send(pack_r, beside.at[0, pl.ds(16, 96)], near, 0, "right"),
        send(pack_l, beside.at[1, pl.ds(16, 96)], near, 1, "left"),
        send(given[0].at[pl.ds(ROWS - 3, 3)], upx, near, 2, "down"),
        send(given[0].at[pl.ds(0, 3)], dnx, near, 3, "up"),
    ]

    def query_of(rows):
        size = len(rows) * COLS
        return q0[:, pl.ds(rows[0] * COLS, size)].reshape(2 * size, D)

    def finish(x, attended, layer):
        x1 = x + dot(attended.astype(BF16), wout[layer])
        inner = dot(norm(x1, mgain[layer : layer + 1]).astype(BF16), win[layer])
        value, gate = inner[:, :FF], inner[:, FF:]
        half = 0.5 * gate * value
        hidden = half + half * jnp.tanh(
            gate * (0.7978845608028654 + (0.7978845608028654 * 0.044715) * (gate * gate))
        )
        return x1 + dot(hidden.astype(BF16), wdown[layer])

    sides = [[] for _ in range(CHUNKS)]
    centres = [[] for _ in range(CHUNKS)]
    relays = [[] for _ in range(CHUNKS)]

    def first_layer(parts, attended):
        tokens = [(i, a, b) for _, _, part in parts for i, a, b in part]
        x = jnp.concatenate([tok[i].astype(F32)[a:b] for i, a, b in tokens], axis=0)
        x = finish(x, jnp.concatenate([attended(i)[a:b] for i, a, b in tokens], axis=0), 0)
        h = norm(x, again[1:2]).astype(BF16)
        at = 0
        for j, start, part in parts:
            size = sum(b - a for _, a, b in part)
            h1[j, pl.ds(start, size)] = h[at : at + size]
            x2[j, pl.ds(start, size)] = x[at : at + size]
            at += size

    def to_side(j, which, at, size, to):
        side, way = (0, "right") if which < 3 else (1, "left")
        sems = (s_far.at[j], r_far.at[j])
        src, part = h1.at[j, pl.ds(at, size)], pl.ds(to, size)
        sides[j].append(send(src, lr.at[0, j, side, part], sems, which, way))

    def to_rows(j, k, at, size):
        sems = (s_far.at[j], r_far.at[j])
        part = pl.ds(at, size)
        centres[j].extend(
            [
                send(h1.at[j, part], rc.at[0, j, part], sems, k, "down"),
                send(h1.at[j, part], rc.at[1, j, part], sems, k + 1, "up"),
            ]
        )

    def own_result(i):
        result = acc0[pl.ds(i * COLS, COLS)]
        return result[:, :D] / result[:, D:]

    def side_results(all_groups):
        attended = {}
        for rows in all_groups:
            i = rows[0]
            first = 2 * ((i + 1) // 2) - 4
            keys = pl.ds((i + 1) // 2 * 16, 64)
            whole = len(rows) == 2
            mask = mside[...] if whole else side_mask(first - i + 3, 1)
            parts = [(k0s[keys], v0s[keys], mask)]
            if i < 3:
                parts.append((k0e[pl.ds(0, 96)], v0e[pl.ds(0, 96)], row_mask(-i, 3, len(rows))))
            if rows[-1] + 4 > ROWS:
                mask = row_mask(ROWS + 3 - i, 3, len(rows))
                parts.append((k0e[pl.ds(96, 96)], v0e[pl.ds(96, 96)], mask))
            result = acc0[pl.ds(i * COLS, len(rows) * COLS)] + attend(query_of(rows), parts)
            result = result[:, :D] / result[:, D:]
            for at, one in enumerate(rows):
                attended[one] = result[at * COLS : (at + 1) * COLS]
        return attended

    def inner_columns():
        inner = [(j, pieces_of(j)[0][1]) for j in range(CHUNKS)]
        first_layer([(j, len(rows) * 8, segments(rows)[1]) for j, rows in inner], own_result)
        for j, rows in inner:
            n = len(rows)
            to_side(j, 0, n * 8, n * 16, n * 8)
            to_side(j, 3, n * 8, n * 16, 0)

    def outer_columns():
        inner = [(j, pieces_of(j)[0][1]) for j in range(CHUNKS)]
        attended = side_results(GROUPS)
        parts = []
        for j, rows in inner:
            segs = segments(rows)
            parts += [(j, 0, segs[0]), (j, len(rows) * 24, segs[2])]
        first_layer(parts, attended.get)
        for j, rows in inner:
            n = len(rows)
            to_side(j, 1, 0, n * 8, 0)
            to_side(j, 4, n * 24, n * 8, n * 16)
        for j, rows in inner:
            to_rows(j, 6, 0, len(rows) * COLS)

    def edge_rows():
        outer = [(j, *pieces_of(j)[1]) for j in range(1, CHUNKS)]
        attended = side_results(EDGE_GROUPS)
        first_layer(
            [(j, first * COLS, sum(segments(rows), [])) for j, first, rows in outer], attended.get
        )
        for j, first, rows in outer:
            n = len(rows)
            to_side(j, 2, first * COLS, n * WIDE, first * WIDE)
            to_side(j, 5, first * COLS + n * 8, n * WIDE, first * WIDE)
        for j, first, rows in outer:
            to_rows(j, 8, first * COLS, len(rows) * COLS)

    for rows in GROUPS + EDGE_GROUPS:
        i, end = rows[0], min(rows[-1] + 4, ROWS)
        begin = max(i - 3, 0)
        keys = pl.ds(begin * COLS, (end - begin) * COLS)
        whole = end - begin == 8
        mask = mown[...] if whole else row_mask(begin - i + 3, end - begin, len(rows))
        acc0[pl.ds(i * COLS, len(rows) * COLS)] = attend(
            query_of(rows), [(k0[keys], v0[keys], mask)]
        )
    inner_columns()
    v0e[pl.ds(0, 96), D:] = jnp.full((96, D), has_up).astype(BF16)
    v0e[pl.ds(96, 96), D:] = jnp.full((96, D), has_down).astype(BF16)
    for d in range(3):
        flags = jnp.concatenate(
            [
                jnp.full((TRIPS * COLS, D), row_ok[d]),
                jnp.full((TRIPS * WIDE, D), row_ok[d] * has_left),
                jnp.full((TRIPS * WIDE, D), row_ok[d] * has_right),
            ],
            axis=0,
        ).astype(BF16)
        for r in range(STEP):
            v1[r, pl.ds(d * BLOCK, BLOCK), D:] = flags

    def halo_keys(x):
        kv = dot(norm(x, again[0:1]).astype(BF16), wqkv[0, :, D:])
        return unit(kv[:, :D], ones).astype(BF16), kv[:, D:]

    def side_tokens(at, size):
        both = [beside[i, pl.ds(at, size)].astype(F32).reshape(size // 8, 8, D) for i in range(2)]
        return jnp.stack(both, axis=1).reshape(2 * size, D)

    def side_ok(size, flag):
        at = lax.broadcasted_iota(jnp.int32, (size, D), 0)
        return jnp.where((at & 8) == 0, has_left, has_right) * flag

    for copy in near_copies[:2]:
        copy.wait_recv()
    near_copies += [
        send(beside.at[:, pl.ds(96, 16)], beside.at[:, pl.ds(0, 16)], near, 4, "down"),
        send(beside.at[:, pl.ds(16, 16)], beside.at[:, pl.ds(112, 16)], near, 5, "up"),
    ]
    key, value = halo_keys(side_tokens(16, 96))
    k0s[pl.ds(32, 192)] = key
    ok = side_ok(192, 1.0)
    v0s[pl.ds(32, 192), :D] = (value * ok).astype(BF16)
    v0s[pl.ds(32, 192), D:] = ok.astype(BF16)

    def far_halo():
        for copy in near_copies[2:]:
            copy.wait_recv()
        x = jnp.concatenate(
            [
                upx[...].astype(F32).reshape(96, D),
                dnx[...].astype(F32).reshape(96, D),
                side_tokens(0, 16),
                side_tokens(112, 16),
            ],
            axis=0,
        )
        key, value = halo_keys(x)
        k0e[...] = key[:192]
        v0e[pl.ds(0, 96), :D] = (value[:96] * has_up).astype(BF16)
        v0e[pl.ds(96, 96), :D] = (value[96:192] * has_down).astype(BF16)
        for at, place, flag in ((192, 0, has_up), (224, 224, has_down)):
            ok = side_ok(32, flag)
            k0s[pl.ds(place, 32)] = key[at : at + 32]
            v0s[pl.ds(place, 32), :D] = (value[at : at + 32] * ok).astype(BF16)
            v0s[pl.ds(place, 32), D:] = ok.astype(BF16)

    def relay(j, k):
        for copy in sides[j][4 * k : 4 + 4 * k]:
            copy.wait_recv()
        sems = (s_far.at[j], r_far.at[j])
        first, rows = pieces_of(j)[k]
        part = pl.ds(first * WIDE, len(rows) * WIDE)
        relays[j] += [
            send(lr.at[0, j, :, part], lr.at[1, j, :, part], sems, 10 + 2 * k, "down"),
            send(lr.at[0, j, :, part], lr.at[2, j, :, part], sems, 11 + 2 * k, "up"),
        ]

    def residues(j):
        firsts = sorted({i % STEP for i in ROWS_OF[j]})
        return [[i + STEP * t for t in range(TRIPS)] for i in firsts]

    def whole_rows(array, j, rows):
        where = place_in(j, ((24, 32), (8, 24), (0, 8)), COLS)
        return [
            array[where[i, a] : where[i, a] + b - a]
            for i in rows
            for a, b in ((0, 8), (8, 24), (24, 32))
        ]

    def far_keys(j, d):
        centre = h1[j] if d == 0 else rc[d - 1, j]
        kv = dot(jnp.concatenate([centre, lr[d, j].reshape(2 * SIDE, D)], axis=0), wqkv[1, :, D:])
        key, value = unit(kv[:, :D], ones), kv[:, D:]
        value = jnp.concatenate(
            [
                value[:TOK] * row_ok[d],
                value[TOK : TOK + SIDE] * (row_ok[d] * has_left),
                value[TOK + SIDE :] * (row_ok[d] * has_right),
            ],
            axis=0,
        )
        on_left = place_in(j, ((24, 32), (8, 24)), WIDE)
        on_right = place_in(j, ((8, 24), (0, 8)), WIDE)
        beside_of = (
            (TOK, on_left, ((8, 24), (24, 32))),
            (TOK + SIDE, on_right, ((0, 8), (8, 24))),
        )
        for r, rows in enumerate(residues(j)):
            for array, ref, lanes in ((key, k1, slice(None)), (value, v1, slice(0, D))):
                piece = jnp.concatenate(
                    whole_rows(array, j, rows)
                    + [
                        array[base + at[i, a] : base + at[i, a] + b - a]
                        for base, at, order in beside_of
                        for i in rows
                        for a, b in order
                    ],
                    axis=0,
                )
                ref[PER * j + r, pl.ds(d * BLOCK, BLOCK), lanes] = piece.astype(BF16)

    def far_own(j):
        q = unit(dot(h1[j], wqkv[1, :, :D]), ones) * query_scale(1)
        far_keys(j, 0)
        for r, rows in enumerate(residues(j)):
            part = jnp.concatenate(whole_rows(q, j, rows), axis=0)
            query = jnp.concatenate([part * low, part * high], axis=0).astype(BF16)
            q1[PER * j + r] = query
            keys = (PER * j + r, pl.ds(0, BLOCK))
            acc1[PER * j + r] = attend(query, [(k1[keys], v1[keys], mfar[:, :BLOCK])])

    def far_layer(j):
        for copy in centres[j] + relays[j]:
            copy.wait_recv()
        far_keys(j, 1)
        far_keys(j, 2)
        attended = {}
        for r, rows in enumerate(residues(j)):
            keys = (PER * j + r, pl.ds(BLOCK, 2 * BLOCK))
            result = acc1[PER * j + r] + attend(
                q1[PER * j + r], [(k1[keys], v1[keys], mfar[:, BLOCK:])]
            )
            result = result[:, :D] / result[:, D:]
            for t, i in enumerate(rows):
                attended[i] = result[t * COLS : (t + 1) * COLS]
        order = [t for _, rows in pieces_of(j) for seg in segments(rows) for t in seg]
        x = finish(x2[j], jnp.concatenate([attended[i][a:b] for i, a, b in order], axis=0), 1)
        for i in ROWS_OF[j]:
            out[i] = jnp.concatenate(whole_rows(x, j, [i]), axis=0).astype(BF16)

    outer_columns()
    far_halo()
    edge_rows()
    for j in range(CHUNKS):
        relay(j, 0)
    far_own(0)
    for j in range(1, CHUNKS):
        relay(j, 1)
    far_layer(0)
    for j in range(1, CHUNKS):
        far_own(j)
    for j in range(1, CHUNKS):
        far_layer(j)
    for copy in near_copies + sum(sides + centres + relays, []):
        copy.wait_send()


def shards(tokens, attn_gain, w_qkv, score_scale, w_out, mlp_gain, w_in, down_weight):
    operands = (tokens, attn_gain, w_qkv, score_scale, w_out, mlp_gain, w_in, down_weight)
    operands = [pltpu.with_memory_space_constraint(a, pltpu.HBM) for a in operands]
    return pl.pallas_call(
        kernel,
        out_shape=jax.ShapeDtypeStruct((ROWS, COLS, D), BF16),
        in_specs=[pl.BlockSpec(memory_space=pltpu.HBM)] * OPERANDS,
        out_specs=pl.BlockSpec(memory_space=pltpu.VMEM),
        scratch_shapes=[pltpu.VMEM(a.shape, a.dtype) for a in operands]
        + [
            pltpu.SemaphoreType.DMA((OPERANDS,)),
            pltpu.VMEM((64, 256), BF16),
            pltpu.VMEM((64, 64), BF16),
            pltpu.VMEM((TRIPS * COLS, 3 * BLOCK), BF16),
            pltpu.VMEM((ROWS * COLS, D), BF16),
            pltpu.VMEM((ROWS * COLS, 2 * D), BF16),
            pltpu.VMEM((192, D), BF16),
            pltpu.VMEM((192, 2 * D), BF16),
            pltpu.VMEM((256, D), BF16),
            pltpu.VMEM((256, 2 * D), BF16),
            pltpu.VMEM((2, ROWS * COLS, D), BF16),
            pltpu.VMEM((ROWS * COLS, 2 * D), F32),
            pltpu.VMEM((CHUNKS, TOK, D), F32),
            pltpu.VMEM((3, COLS, D), BF16),
            pltpu.VMEM((3, COLS, D), BF16),
            pltpu.VMEM((96, D), BF16),
            pltpu.VMEM((96, D), BF16),
            pltpu.VMEM((2, 128, D), BF16),
            pltpu.VMEM((CHUNKS, TOK, D), BF16),
            pltpu.VMEM((2, CHUNKS, TOK, D), BF16),
            pltpu.VMEM((3, CHUNKS, 2, SIDE, D), BF16),
            pltpu.VMEM((STEP, 2 * TRIPS * COLS, D), BF16),
            pltpu.VMEM((STEP, 3 * BLOCK, D), BF16),
            pltpu.VMEM((STEP, 3 * BLOCK, 2 * D), BF16),
            pltpu.VMEM((STEP, TRIPS * COLS, 2 * D), F32),
            pltpu.SemaphoreType.DMA((6,)),
            pltpu.SemaphoreType.DMA((6,)),
            pltpu.SemaphoreType.DMA((CHUNKS, 14)),
            pltpu.SemaphoreType.DMA((CHUNKS, 14)),
        ],
        compiler_params=pltpu.CompilerParams(
            collective_id=0, has_side_effects=True, vmem_limit_bytes=48 * 1024 * 1024
        ),
        name="two_layers",
    )(*operands)


def solution(mesh):
    return jax.shard_map(
        shards,
        mesh=mesh,
        in_specs=(P("row", "col", None), P(), P(), P(), P(), P(), P(), P()),
        out_specs=P("row", "col", None),
        check_vma=False,
    )
```

time: 33.2 us -> 31.5 us (0.949)
  the two profiles are of different devices: /device:TPU:64 before, /device:TPU:24 now
where the time goes in v4:
time: 31.5 us; the launch traced here: 31.2 us
  Pallas kernels  30.5 us (97%)
  local copies, waits for them, and re-layouts  0.68 us (2%)
    pallas_call x1, Pallas kernels, shards(): pl.pallas_call(kernel, out_shape=jax.ShapeDtypeStruct((ROWS, COLS, D), BF...  30.5 us
    unnamed x1, local copies, waits for them, and re-layouts  0.68 us

profile of v4, /device:TPU:24, one launch (start us, length us, event | category | flops | bytes accessed | tf_op | source)
XLA Modules:
  0.0 31.2 jit_solution(16780860139571592376)
XLA Ops:
  0.0 30.5 %two_layers.1 = bf16[24,32,128]{2,1,0:T(8,128)(2,1)S(1)} custom-call(bf16[24,32,128]{2,1,0:T(8,128)(2,1)} %refs_0_.1, f32[2,128]{1,0:T(2,128)} %refs_1_.1, bf16[2,128,384]{2,1,0:T(8,128)(2,1)} %refs_2_.1, f32[2,2]{1,0:T(2,128)} %refs_3_.1, bf16[2,128,128]{2,1,0:T(8,128)(2,1)} %refs_4_.1, f32[2,128]{1,0:T(2,128)} %refs_5_.1, bf16[2,128,768]{2,1,0:T(8,128)(2,1)} %refs_6_.1, ...), custom_call_target="tpu_custom_call" | custom-call | tf_op jit(solution)/shard_map/two_layers/pallas_call | solution.py:516
  30.6 0.7 %copy.10 = bf16[24,32,128]{2,1,0:T(8,128)(2,1)} copy(bf16[24,32,128]{2,1,0:T(8,128)(2,1)S(1)} %two_layers.1) | data formatting | bytes 393216

commit v5 on v4

--- a/solution.py
+++ b/solution.py
@@ -98,8 +98,12 @@
     return x * lax.rsqrt(jnp.mean(x * x, axis=-1, keepdims=True) + 1e-6) * gain
 
 
-def unit(x, ones):
-    return x * lax.rsqrt(dot((x * x).astype(BF16), ones) + 1e-6)
+def unit(x):
+    first = lax.broadcasted_iota(jnp.int32, (1, D), 1) < D // 2
+    square = x * x
+    low = jnp.sum(jnp.where(first, square, 0.0), axis=-1, keepdims=True)
+    high = jnp.sum(jnp.where(first, 0.0, square), axis=-1, keepdims=True)
+    return x * jnp.where(first, lax.rsqrt(low + 1e-6), lax.rsqrt(high + 1e-6))
 
 
 OPERANDS = 8
@@ -173,32 +177,34 @@
         .astype(BF16)
     )
 
-    class Message:
-        def __init__(self, src, dst, sems, at, way):
-            self.copy = pltpu.make_async_remote_copy(
-                src_ref=src, dst_ref=dst, send_sem=sems[0].at[at], recv_sem=sems[1].at[at],
-                device_id=device_at[way], device_id_type=MESH,
-            )
-            self.sends, self.receives = exists[way], exists[opposite[way]]
-            pl.when(self.sends)(self.copy.start)
-
-        def wait_recv(self):
-            pl.when(self.receives)(self.copy.wait_recv)
-
-        def wait_send(self):
-            pl.when(self.sends)(self.copy.wait_send)
-
-    send = Message
+    def send(src, dst, sems, at, way):
+        copy = pltpu.make_async_remote_copy(
+            src_ref=src, dst_ref=dst, send_sem=sems[0].at[at], recv_sem=sems[1].at[at],
+            device_id=device_at[way], device_id_type=MESH,
+        )
+        return way, copy
+
+    def each(copies, act, receiving=False):
+        for way in ("right", "left", "down", "up"):
+            mine = [copy for to, copy in copies if to == way]
+            if mine:
+
+                @pl.when(exists[opposite[way] if receiving else way])
+                def _(mine=mine):
+                    for copy in mine:
+                        act(copy)
+
+    def start(copies):
+        each(copies, lambda copy: copy.start())
+        return copies
+
+    def received(copies):
+        each(copies, lambda copy: copy.wait_recv(), receiving=True)
 
     lane = lax.broadcasted_iota(jnp.int32, (1, 2 * D), 1)
     first_head = (lane & (D // 2)) == 0
     low = jnp.where(first_head[:, :D], 1.0, 0.0)
     high = 1.0 - low
-    same = (lax.broadcasted_iota(jnp.int32, (D, D), 0) < D // 2) == (
-        lax.broadcasted_iota(jnp.int32, (D, D), 1) < D // 2
-    )
-    ones = jnp.where(same, 1.0, 0.0).astype(BF16)
-
     def query_scale(layer):
         scale = sscale[layer : layer + 1]
         return (scale[:, :1] * low + scale[:, 1:] * high) * LOG2E
@@ -217,21 +223,21 @@
         return jnp.where(first_head, total[:size], total[size:])
 
     qkv = dot(norm(x0.reshape(ROWS * COLS, D), again[0:1]).astype(BF16), wqkv[0])
-    q = unit(qkv[:, :D], ones) * query_scale(0)
+    q = unit(qkv[:, :D]) * query_scale(0)
     q0[0] = (q * low).astype(BF16)
     q0[1] = (q * high).astype(BF16)
-    k0[...] = unit(qkv[:, D : 2 * D], ones).astype(BF16)
+    k0[...] = unit(qkv[:, D : 2 * D]).astype(BF16)
     v0[:, :D] = qkv[:, 2 * D :].astype(BF16)
     v0[:, D:] = jnp.ones((ROWS * COLS, D), BF16)
 
     pl.semaphore_wait(barrier, greeted)
     near = (s_near, r_near)
-    near_copies = [
+    near_copies = start([
         send(pack_r, beside.at[0, pl.ds(16, 96)], near, 0, "right"),
         send(pack_l, beside.at[1, pl.ds(16, 96)], near, 1, "left"),
         send(given[0].at[pl.ds(ROWS - 3, 3)], upx, near, 2, "down"),
         send(given[0].at[pl.ds(0, 3)], dnx, near, 3, "up"),
-    ]
+    ])
 
     def query_of(rows):
         size = len(rows) * COLS
@@ -262,6 +268,13 @@
             h1[j, pl.ds(start, size)] = h[at : at + size]
             x2[j, pl.ds(start, size)] = x[at : at + size]
             at += size
+
+    begun = []
+
+    def fresh():
+        new = [c for c in sum(sides + centres + relays, []) if not any(c is b for b in begun)]
+        begun.extend(new)
+        return new
 
     def to_side(j, which, at, size, to):
         side, way = (0, "right") if which < 3 else (1, "left")
@@ -310,6 +323,7 @@
             n = len(rows)
             to_side(j, 0, n * 8, n * 16, n * 8)
             to_side(j, 3, n * 8, n * 16, 0)
+        start(fresh())
 
     def outer_columns():
         inner = [(j, pieces_of(j)[0][1]) for j in range(CHUNKS)]
@@ -325,6 +339,7 @@
             to_side(j, 4, n * 24, n * 8, n * 16)
         for j, rows in inner:
             to_rows(j, 6, 0, len(rows) * COLS)
+        start(fresh())
 
     def edge_rows():
         outer = [(j, *pieces_of(j)[1]) for j in range(1, CHUNKS)]
@@ -338,6 +353,7 @@
             to_side(j, 5, first * COLS + n * 8, n * WIDE, first * WIDE)
         for j, first, rows in outer:
             to_rows(j, 8, first * COLS, len(rows) * COLS)
+        start(fresh())
 
     for rows in GROUPS + EDGE_GROUPS:
         i, end = rows[0], min(rows[-1] + 4, ROWS)
@@ -365,7 +381,7 @@
 
     def halo_keys(x):
         kv = dot(norm(x, again[0:1]).astype(BF16), wqkv[0, :, D:])
-        return unit(kv[:, :D], ones).astype(BF16), kv[:, D:]
+        return unit(kv[:, :D]).astype(BF16), kv[:, D:]
 
     def side_tokens(at, size):
         both = [beside[i, pl.ds(at, size)].astype(F32).reshape(size // 8, 8, D) for i in range(2)]
@@ -375,21 +391,19 @@
         at = lax.broadcasted_iota(jnp.int32, (size, D), 0)
         return jnp.where((at & 8) == 0, has_left, has_right) * flag
 
-    for copy in near_copies[:2]:
-        copy.wait_recv()
-    near_copies += [
+    received(near_copies[:2])
+    near_copies += start([
         send(beside.at[:, pl.ds(96, 16)], beside.at[:, pl.ds(0, 16)], near, 4, "down"),
         send(beside.at[:, pl.ds(16, 16)], beside.at[:, pl.ds(112, 16)], near, 5, "up"),
-    ]
+    ])
     key, value = halo_keys(side_tokens(16, 96))
     k0s[pl.ds(32, 192)] = key
     ok = side_ok(192, 1.0)
-    v0s[pl.ds(32, 192), :D] = (value * ok).astype(BF16)
+    v0s[pl.ds(32, 192), :D] = value.astype(BF16)
     v0s[pl.ds(32, 192), D:] = ok.astype(BF16)
 
     def far_halo():
-        for copy in near_copies[2:]:
-            copy.wait_recv()
+        received(near_copies[2:])
         x = jnp.concatenate(
             [
                 upx[...].astype(F32).reshape(96, D),
@@ -401,24 +415,25 @@
         )
         key, value = halo_keys(x)
         k0e[...] = key[:192]
-        v0e[pl.ds(0, 96), :D] = (value[:96] * has_up).astype(BF16)
-        v0e[pl.ds(96, 96), :D] = (value[96:192] * has_down).astype(BF16)
+        v0e[pl.ds(0, 96), :D] = value[:96].astype(BF16)
+        v0e[pl.ds(96, 96), :D] = value[96:192].astype(BF16)
         for at, place, flag in ((192, 0, has_up), (224, 224, has_down)):
             ok = side_ok(32, flag)
             k0s[pl.ds(place, 32)] = key[at : at + 32]
-            v0s[pl.ds(place, 32), :D] = (value[at : at + 32] * ok).astype(BF16)
+            v0s[pl.ds(place, 32), :D] = value[at : at + 32].astype(BF16)
             v0s[pl.ds(place, 32), D:] = ok.astype(BF16)
 
-    def relay(j, k):
-        for copy in sides[j][4 * k : 4 + 4 * k]:
-            copy.wait_recv()
-        sems = (s_far.at[j], r_far.at[j])
-        first, rows = pieces_of(j)[k]
-        part = pl.ds(first * WIDE, len(rows) * WIDE)
-        relays[j] += [
-            send(lr.at[0, j, :, part], lr.at[1, j, :, part], sems, 10 + 2 * k, "down"),
-            send(lr.at[0, j, :, part], lr.at[2, j, :, part], sems, 11 + 2 * k, "up"),
-        ]
+    def relay(chunks, k):
+        received(sum([sides[j][4 * k : 4 + 4 * k] for j in chunks], []))
+        for j in chunks:
+            sems = (s_far.at[j], r_far.at[j])
+            first, rows = pieces_of(j)[k]
+            part = pl.ds(first * WIDE, len(rows) * WIDE)
+            relays[j] += [
+                send(lr.at[0, j, :, part], lr.at[1, j, :, part], sems, 10 + 2 * k, "down"),
+                send(lr.at[0, j, :, part], lr.at[2, j, :, part], sems, 11 + 2 * k, "up"),
+            ]
+        start(fresh())
 
     def residues(j):
         firsts = sorted({i % STEP for i in ROWS_OF[j]})
@@ -435,15 +450,7 @@
     def far_keys(j, d):
         centre = h1[j] if d == 0 else rc[d - 1, j]
         kv = dot(jnp.concatenate([centre, lr[d, j].reshape(2 * SIDE, D)], axis=0), wqkv[1, :, D:])
-        key, value = unit(kv[:, :D], ones), kv[:, D:]
-        value = jnp.concatenate(
-            [
-                value[:TOK] * row_ok[d],
-                value[TOK : TOK + SIDE] * (row_ok[d] * has_left),
-                value[TOK + SIDE :] * (row_ok[d] * has_right),
-            ],
-            axis=0,
-        )
+        key, value = unit(kv[:, :D]), kv[:, D:]
         on_left = place_in(j, ((24, 32), (8, 24)), WIDE)
         on_right = place_in(j, ((8, 24), (0, 8)), WIDE)
         beside_of = (
@@ -465,7 +472,7 @@
                 ref[PER * j + r, pl.ds(d * BLOCK, BLOCK), lanes] = piece.astype(BF16)
 
     def far_own(j):
-        q = unit(dot(h1[j], wqkv[1, :, :D]), ones) * query_scale(1)
+        q = unit(dot(h1[j], wqkv[1, :, :D])) * query_scale(1)
         far_keys(j, 0)
         for r, rows in enumerate(residues(j)):
             part = jnp.concatenate(whole_rows(q, j, rows), axis=0)
@@ -475,8 +482,6 @@
             acc1[PER * j + r] = attend(query, [(k1[keys], v1[keys], mfar[:, :BLOCK])])
 
     def far_layer(j):
-        for copy in centres[j] + relays[j]:
-            copy.wait_recv()
         far_keys(j, 1)
         far_keys(j, 2)
         attended = {}
@@ -496,18 +501,19 @@
     outer_columns()
     far_halo()
     edge_rows()
-    for j in range(CHUNKS):
-        relay(j, 0)
+    last = range(1, CHUNKS)
+    relay([0], 0)
+    relay(last, 0)
     far_own(0)
-    for j in range(1, CHUNKS):
-        relay(j, 1)
+    relay(last, 1)
+    received(centres[0] + relays[0])
     far_layer(0)
-    for j in range(1, CHUNKS):
+    for j in last:
         far_own(j)
-    for j in range(1, CHUNKS):
+    received(sum([centres[j] + relays[j] for j in last], []))
+    for j in last:
         far_layer(j)
-    for copy in near_copies + sum(sides + centres + relays, []):
-        copy.wait_send()
+    each(near_copies + sum(sides + centres + relays, []), lambda copy: copy.wait_send())
 
 
 def shards(tokens, attn_gain, w_qkv, score_scale, w_out, mlp_gain, w_in, down_weight):

time: 31.5 us -> 30.4 us (0.965)
  Pallas kernels: 30.5 us -> 29.6 us
    pallas_call x1, Pallas kernels: 30.5 us -> 29.6 us  [shards(): pl.pallas_call(kernel, out_shape=jax.ShapeDtypeStruct((ROWS, COLS, D), BF...]
where the time goes in v5:
time: 30.4 us; the launch traced here: 30.3 us
  Pallas kernels  29.6 us (97%)
  local copies, waits for them, and re-layouts  0.68 us (2%)
    pallas_call x1, Pallas kernels, shards(): pl.pallas_call(kernel, out_shape=jax.ShapeDtypeStruct((ROWS, COLS, D), BF...  29.6 us
    unnamed x1, local copies, waits for them, and re-layouts  0.68 us

profile of v5, /device:TPU:24, one launch (start us, length us, event | category | flops | bytes accessed | tf_op | source)
XLA Modules:
  0.0 30.3 jit_solution(14755027352522334029)
XLA Ops:
  0.0 29.6 %two_layers.1 = bf16[24,32,128]{2,1,0:T(8,128)(2,1)S(1)} custom-call(bf16[24,32,128]{2,1,0:T(8,128)(2,1)} %refs_0_.1, f32[2,128]{1,0:T(2,128)} %refs_1_.1, bf16[2,128,384]{2,1,0:T(8,128)(2,1)} %refs_2_.1, f32[2,2]{1,0:T(2,128)} %refs_3_.1, bf16[2,128,128]{2,1,0:T(8,128)(2,1)} %refs_4_.1, f32[2,128]{1,0:T(2,128)} %refs_5_.1, bf16[2,128,768]{2,1,0:T(8,128)(2,1)} %refs_6_.1, ...), custom_call_target="tpu_custom_call" | custom-call | tf_op jit(solution)/shard_map/two_layers/pallas_call | solution.py:522
  29.6 0.7 %copy.10 = bf16[24,32,128]{2,1,0:T(8,128)(2,1)} copy(bf16[24,32,128]{2,1,0:T(8,128)(2,1)S(1)} %two_layers.1) | data formatting | bytes 393216

commit v6 on v5

--- a/solution.py
+++ b/solution.py
@@ -447,10 +447,17 @@
             for a, b in ((0, 8), (8, 24), (24, 32))
         ]
 
-    def far_keys(j, d):
-        centre = h1[j] if d == 0 else rc[d - 1, j]
-        kv = dot(jnp.concatenate([centre, lr[d, j].reshape(2 * SIDE, D)], axis=0), wqkv[1, :, D:])
-        key, value = unit(kv[:, :D]), kv[:, D:]
+    def far_keys(wanted):
+        tokens = []
+        for j, d in wanted:
+            tokens += [h1[j] if d == 0 else rc[d - 1, j], lr[d, j].reshape(2 * SIDE, D)]
+        kv = dot(jnp.concatenate(tokens, axis=0), wqkv[1, :, D:])
+        keys, values = unit(kv[:, :D]), kv[:, D:]
+        for at, (j, d) in enumerate(wanted):
+            part = slice(at * (TOK + 2 * SIDE), (at + 1) * (TOK + 2 * SIDE))
+            keep_keys(j, d, keys[part], values[part])
+
+    def keep_keys(j, d, key, value):
         on_left = place_in(j, ((24, 32), (8, 24)), WIDE)
         on_right = place_in(j, ((8, 24), (0, 8)), WIDE)
         beside_of = (
@@ -471,32 +478,40 @@
                 )
                 ref[PER * j + r, pl.ds(d * BLOCK, BLOCK), lanes] = piece.astype(BF16)
 
-    def far_own(j):
-        q = unit(dot(h1[j], wqkv[1, :, :D])) * query_scale(1)
-        far_keys(j, 0)
-        for r, rows in enumerate(residues(j)):
-            part = jnp.concatenate(whole_rows(q, j, rows), axis=0)
-            query = jnp.concatenate([part * low, part * high], axis=0).astype(BF16)
-            q1[PER * j + r] = query
-            keys = (PER * j + r, pl.ds(0, BLOCK))
-            acc1[PER * j + r] = attend(query, [(k1[keys], v1[keys], mfar[:, :BLOCK])])
-
-    def far_layer(j):
-        far_keys(j, 1)
-        far_keys(j, 2)
-        attended = {}
-        for r, rows in enumerate(residues(j)):
-            keys = (PER * j + r, pl.ds(BLOCK, 2 * BLOCK))
-            result = acc1[PER * j + r] + attend(
-                q1[PER * j + r], [(k1[keys], v1[keys], mfar[:, BLOCK:])]
-            )
-            result = result[:, :D] / result[:, D:]
-            for t, i in enumerate(rows):
-                attended[i] = result[t * COLS : (t + 1) * COLS]
-        order = [t for _, rows in pieces_of(j) for seg in segments(rows) for t in seg]
-        x = finish(x2[j], jnp.concatenate([attended[i][a:b] for i, a, b in order], axis=0), 1)
-        for i in ROWS_OF[j]:
-            out[i] = jnp.concatenate(whole_rows(x, j, [i]), axis=0).astype(BF16)
+    def far_own(chunks):
+        q = unit(dot(jnp.concatenate([h1[j] for j in chunks], axis=0), wqkv[1, :, :D]))
+        q = q * query_scale(1)
+        far_keys([(j, 0) for j in chunks])
+        for at, j in enumerate(chunks):
+            for r, rows in enumerate(residues(j)):
+                part = whole_rows(q[at * TOK : (at + 1) * TOK], j, rows)
+                part = jnp.concatenate(part, axis=0)
+                query = jnp.concatenate([part * low, part * high], axis=0).astype(BF16)
+                q1[PER * j + r] = query
+                keys = (PER * j + r, pl.ds(0, BLOCK))
+                acc1[PER * j + r] = attend(query, [(k1[keys], v1[keys], mfar[:, :BLOCK])])
+
+    def far_layer(chunks):
+        attended = []
+        far_keys([(j, d) for j in chunks for d in (1, 2)])
+        for j in chunks:
+            found = {}
+            for r, rows in enumerate(residues(j)):
+                keys = (PER * j + r, pl.ds(BLOCK, 2 * BLOCK))
+                result = acc1[PER * j + r] + attend(
+                    q1[PER * j + r], [(k1[keys], v1[keys], mfar[:, BLOCK:])]
+                )
+                result = result[:, :D] / result[:, D:]
+                for t, i in enumerate(rows):
+                    found[i] = result[t * COLS : (t + 1) * COLS]
+            order = [t for _, rows in pieces_of(j) for seg in segments(rows) for t in seg]
+            attended += [found[i][a:b] for i, a, b in order]
+        x = jnp.concatenate([x2[j] for j in chunks], axis=0)
+        x = finish(x, jnp.concatenate(attended, axis=0), 1)
+        for at, j in enumerate(chunks):
+            for i in ROWS_OF[j]:
+                rows = whole_rows(x[at * TOK : (at + 1) * TOK], j, [i])
+                out[i] = jnp.concatenate(rows, axis=0).astype(BF16)
 
     outer_columns()
     far_halo()
@@ -504,15 +519,13 @@
     last = range(1, CHUNKS)
     relay([0], 0)
     relay(last, 0)
-    far_own(0)
+    far_own([0])
     relay(last, 1)
     received(centres[0] + relays[0])
-    far_layer(0)
-    for j in last:
-        far_own(j)
+    far_layer([0])
+    far_own(last)
     received(sum([centres[j] + relays[j] for j in last], []))
-    for j in last:
-        far_layer(j)
+    far_layer(last)
     each(near_copies + sum(sides + centres + relays, []), lambda copy: copy.wait_send())
 
 

time: 30.4 us -> 28.7 us (0.944)
  Pallas kernels: 29.6 us -> 27.9 us
    pallas_call x1, Pallas kernels: 29.6 us -> 27.9 us  [shards(): pl.pallas_call(kernel, out_shape=jax.ShapeDtypeStruct((ROWS, COLS, D), BF...]
where the time goes in v6:
time: 28.7 us; the launch traced here: 28.6 us
  Pallas kernels  27.9 us (97%)
  local copies, waits for them, and re-layouts  0.68 us (2%)
    pallas_call x1, Pallas kernels, shards(): pl.pallas_call(kernel, out_shape=jax.ShapeDtypeStruct((ROWS, COLS, D), BF...  27.9 us
    unnamed x1, local copies, waits for them, and re-layouts  0.68 us

profile of v6, /device:TPU:24, one launch (start us, length us, event | category | flops | bytes accessed | tf_op | source)
XLA Modules:
  0.0 28.6 jit_solution(11166192213997776022)
XLA Ops:
  0.0 27.9 %two_layers.1 = bf16[24,32,128]{2,1,0:T(8,128)(2,1)S(1)} custom-call(bf16[24,32,128]{2,1,0:T(8,128)(2,1)} %refs_0_.1, f32[2,128]{1,0:T(2,128)} %refs_1_.1, bf16[2,128,384]{2,1,0:T(8,128)(2,1)} %refs_2_.1, f32[2,2]{1,0:T(2,128)} %refs_3_.1, bf16[2,128,128]{2,1,0:T(8,128)(2,1)} %refs_4_.1, f32[2,128]{1,0:T(2,128)} %refs_5_.1, bf16[2,128,768]{2,1,0:T(8,128)(2,1)} %refs_6_.1, ...), custom_call_target="tpu_custom_call" | custom-call | tf_op jit(solution)/shard_map/two_layers/pallas_call | solution.py:535
  27.9 0.7 %copy.10 = bf16[24,32,128]{2,1,0:T(8,128)(2,1)} copy(bf16[24,32,128]{2,1,0:T(8,128)(2,1)S(1)} %two_layers.1) | data formatting | bytes 393216

commit v7 on v6

--- a/solution.py
+++ b/solution.py
@@ -16,6 +16,7 @@
 ROWS_OF = ((3, 11, 19, 4, 12, 20), (9, 17, 10, 18, 1, 2), (5, 13, 6, 14, 21, 22), (7, 15, 8, 16, 23, 0))
 EDGE = (0, 1, 2, 21, 22, 23)
 GROUPS = ((3, 4), (11, 12), (19, 20), (9, 10), (17, 18), (5, 6), (13, 14), (7, 8), (15, 16))
+SIDE_GROUPS = ((3, 4, 5, 6), (7, 8, 9, 10), (11, 12, 13, 14), (15, 16, 17, 18), (19, 20))
 EDGE_GROUPS = ((1, 2), (21, 22), (23,), (0,))
 CHUNKS = 4
 PER = STEP // CHUNKS
@@ -63,7 +64,7 @@
 
 
 def side_mask(first, queries=2):
-    a, c, n = lanes_and_rows(queries * COLS, 64)
+    a, c, n = lanes_and_rows(queries * COLS, 80 if queries == 4 else 64)
     step = 2 * (n >> 4) + ((n >> 2) & 1) + first - a
     at = (n & 3) + jnp.where((n & 8) == 0, -4, COLS)
     return as_mask((step >= 0) & (step <= 6) & (abs(at - c) <= 3))
@@ -115,7 +116,7 @@
 
 def body(
     given, out,
-    tok, again, wqkv, sscale, wout, mgain, win, wdown, s_given, mown, mside, mfar,
+    tok, again, wqkv, sscale, wout, mgain, win, wdown, s_given, mown, mside, mside4, mfar,
     k0, v0, k0e, v0e, k0s, v0s, q0, acc0, x2, upx, dnx, pack_l, pack_r, beside,
     h1, rc, lr, q1, k1, v1, acc1, s_near, r_near, s_far, r_far,
 ):
@@ -162,6 +163,7 @@
 
     mown[...] = row_mask(0, 8)
     mside[...] = side_mask(0)
+    mside4[...] = side_mask(0, 4)
     mfar[...] = far_mask()
 
     fetches[0].wait()
@@ -301,9 +303,11 @@
         for rows in all_groups:
             i = rows[0]
             first = 2 * ((i + 1) // 2) - 4
-            keys = pl.ds((i + 1) // 2 * 16, 64)
-            whole = len(rows) == 2
-            mask = mside[...] if whole else side_mask(first - i + 3, 1)
+            keys = pl.ds((i + 1) // 2 * 16, 80 if len(rows) == 4 else 64)
+            if len(rows) == 1:
+                mask = side_mask(first - i + 3, 1)
+            else:
+                mask = mside[...] if len(rows) == 2 else mside4[...]
             parts = [(k0s[keys], v0s[keys], mask)]
             if i < 3:
                 parts.append((k0e[pl.ds(0, 96)], v0e[pl.ds(0, 96)], row_mask(-i, 3, len(rows))))
@@ -327,7 +331,7 @@
 
     def outer_columns():
         inner = [(j, pieces_of(j)[0][1]) for j in range(CHUNKS)]
-        attended = side_results(GROUPS)
+        attended = side_results(SIDE_GROUPS)
         parts = []
         for j, rows in inner:
             segs = segments(rows)
@@ -542,6 +546,7 @@
             pltpu.SemaphoreType.DMA((OPERANDS,)),
             pltpu.VMEM((64, 256), BF16),
             pltpu.VMEM((64, 64), BF16),
+            pltpu.VMEM((128, 80), BF16),
             pltpu.VMEM((TRIPS * COLS, 3 * BLOCK), BF16),
             pltpu.VMEM((ROWS * COLS, D), BF16),
             pltpu.VMEM((ROWS * COLS, 2 * D), BF16),

time: 28.7 us -> 28.6 us (level)
  no operation moved by 1% of the time
where the time goes in v7:
time: 28.6 us; the launch traced here: 28.5 us
  Pallas kernels  27.9 us (98%)
  local copies, waits for them, and re-layouts  0.68 us (2%)
    pallas_call x1, Pallas kernels, shards(): pl.pallas_call(kernel, out_shape=jax.ShapeDtypeStruct((ROWS, COLS, D), BF...  27.9 us
    unnamed x1, local copies, waits for them, and re-layouts  0.68 us

profile of v7, /device:TPU:24, one launch (start us, length us, event | category | flops | bytes accessed | tf_op | source)
XLA Modules:
  0.0 28.5 jit_solution(3882590339452499370)
XLA Ops:
  0.0 27.9 %two_layers.1 = bf16[24,32,128]{2,1,0:T(8,128)(2,1)S(1)} custom-call(bf16[24,32,128]{2,1,0:T(8,128)(2,1)} %refs_0_.1, f32[2,128]{1,0:T(2,128)} %refs_1_.1, bf16[2,128,384]{2,1,0:T(8,128)(2,1)} %refs_2_.1, f32[2,2]{1,0:T(2,128)} %refs_3_.1, bf16[2,128,128]{2,1,0:T(8,128)(2,1)} %refs_4_.1, f32[2,128]{1,0:T(2,128)} %refs_5_.1, bf16[2,128,768]{2,1,0:T(8,128)(2,1)} %refs_6_.1, ...), custom_call_target="tpu_custom_call" | custom-call | tf_op jit(solution)/shard_map/two_layers/pallas_call | solution.py:539
  27.9 0.7 %copy.10 = bf16[24,32,128]{2,1,0:T(8,128)(2,1)} copy(bf16[24,32,128]{2,1,0:T(8,128)(2,1)S(1)} %two_layers.1) | data formatting | bytes 393216
